TPU v7x, 32 devices: a whole 2x2x4 slice. The times are simulated.
32 devices in a mesh: tok: 8 (over y, x, core), head: 4 (over z).
Axes of the slice: x: 2, y: 2, z: 4, core: 2. Of those that a mesh axis runs over, the one named last changes fastest.
Arguments:
- tokens: bfloat16 [2048, 1024], P('tok'), may hold values from -6 to 6
- class_ids: int32 [3], replicated, may hold values from 0 to 999
- slot_item: int32 [2048], replicated, may hold values from -1 to 2, as said below
- slot_scale: int32 [2048], replicated, may hold values from 0 to 9, as said below
- class_table: bfloat16 [1000, 1024], replicated, may hold values from -6 to 6
- w_ada: bfloat16 [6, 1024, 1024], replicated, may hold values from -0.1875 to 0.1875
- w_qkv: bfloat16 [1024, 3, 1024], P(None, None, 'head'), may hold values from -0.1875 to 0.1875
- w_out: bfloat16 [1024, 1024], P('head'), may hold values from -2 to 2
- w_fc1: bfloat16 [1024, 4096], P(None, 'head'), may hold values from -0.1875 to 0.1875
- w_fc2: bfloat16 [4096, 1024], P('head'), may hold values from -0.09375 to 0.09375
- cotangent: bfloat16 [2048, 1024], P('tok'), may hold values from -6 to 6
Outputs:
- output: bfloat16 [2048, 1024], P('tok')
- d_tokens: bfloat16 [2048, 1024], P('tok')
- d_class_table: float32 [1000, 1024], P(None, 'head')
- d_w_ada: float32 [6, 1024, 1024], P(None, None, 'head')
- d_w_qkv: float32 [1024, 3, 1024], P(None, None, 'head')
- d_w_out: float32 [1024, 1024], P('head')
- d_w_fc1: float32 [1024, 4096], P(None, 'head')
- d_w_fc2: float32 [4096, 1024], P('head')
Inputs may be any that keep to these rules, and one draw needn't show every extreme that they name: `slot_item`: empty slots hold -1, the others an image. All tokens of scale s of all images precede those of scale s + 1; scale s of an image holds p * p tokens in a row, p = 1, 2, 3, 4, 5, 6, 8, 10, 13, 16 for s = 0 to 9; every image has all its 680 tokens; empty slots lie anywhere. `slot_scale`: the scale of the slot's token; an empty slot repeats the scale of the nearest earlier token (0 before the first), so the values never fall along the slots.
All inputs are finite; a program needn't handle non-finite values.
Results may differ from a plain program's by a relative error of at most 0.018.
Values may be sent and summed in bfloat16 or wider, within the bound.
A program may use at most 192 MiB of HBM per device.

v0:
```python
import math

import jax
import jax.numpy as jnp
from jax import lax
from jax.sharding import PartitionSpec as P

HEAD_DIM = 64


EPS = 1e-06
HIGH = lax.Precision.HIGHEST


def layer_norm(values):
    centre = jnp.mean(values, axis=-1, keepdims=True)
    shifted = values - centre
    spread = jnp.mean(shifted * shifted, axis=-1, keepdims=True)
    return shifted * lax.rsqrt(spread + EPS)


def modulate(values, scale_in, shift_in):
    return layer_norm(values) * (1.0 + scale_in) + shift_in


def pair_scores(queries, key_block, query_item, key_item, query_scale, key_scale):
    scores = (
        jnp.einsum("qhd,khd->hqk", queries, key_block, preferred_element_type=jnp.float32) * 0.125
    )
    allowed = (
        (query_item[:, None] == key_item[None, :]) & (key_scale[None, :] <= query_scale[:, None])
    )[None]
    return (jnp.where(allowed, scores, -1e30), allowed)


def on_device(
    tokens,
    class_ids,
    slot_item,
    slot_scale,
    class_table,
    w_ada,
    w_qkv,
    w_out,
    w_fc1,
    w_fc2,
    cotangent,
):
    tok_rows, full_width = tokens.shape
    slot_count = slot_item.shape[0]
    item_count = class_ids.shape[0]
    class_count = class_table.shape[0]
    local_width = w_qkv.shape[2]
    local_heads = local_width // HEAD_DIM
    anchor = lax.axis_index("tok") * tok_rows
    first_col = lax.axis_index("head") * local_width
    my_item = lax.dynamic_slice_in_dim(slot_item, anchor, tok_rows)
    my_scale = lax.dynamic_slice_in_dim(slot_scale, anchor, tok_rows)
    class_pick = (class_ids[:, None] == jnp.arange(class_count, dtype=jnp.int32)[None, :]).astype(
        jnp.bfloat16
    )
    cond = jnp.dot(class_pick, class_table, preferred_element_type=jnp.float32)
    silu_cond, silu_back = jax.vjp(jax.nn.silu, cond)
    cond_low = silu_cond.astype(jnp.bfloat16)
    modes = jnp.einsum("id,cde->ice", cond_low, w_ada, preferred_element_type=jnp.float32)
    item_pick = (my_item[:, None] == jnp.arange(item_count, dtype=jnp.int32)[None, :]).astype(
        jnp.float32
    )
    per_token = jnp.dot(
        item_pick, modes.reshape(item_count, 6 * full_width), precision=HIGH
    ).reshape(tok_rows, 6, full_width)
    gamma_one = per_token[:, 0]
    gamma_two = per_token[:, 1]
    scale_one = per_token[:, 2]
    scale_two = per_token[:, 3]
    shift_one = per_token[:, 4]
    shift_two = per_token[:, 5]
    tok_float = tokens.astype(jnp.float32)
    a_pre, a_back = jax.vjp(modulate, tok_float, scale_one, shift_one)
    a_low = a_pre.astype(jnp.bfloat16)
    qkv_low = jnp.einsum("td,dce->tce", a_low, w_qkv, preferred_element_type=jnp.float32).astype(
        jnp.bfloat16
    )
    queries = qkv_low[:, 0]
    key_own = qkv_low[:, 1]
    value_own = qkv_low[:, 2]
    query_heads = queries.reshape(tok_rows, local_heads, HEAD_DIM)
    key_all, value_all = (
        lax.all_gather(key_own, "tok", axis=0, tiled=True),
        lax.all_gather(value_own, "tok", axis=0, tiled=True),
    )
    block_rows = math.gcd(slot_count, 2048)
    blocks = slot_count // block_rows
    key_blocks = key_all.reshape(blocks, block_rows, local_heads, HEAD_DIM)
    value_blocks = value_all.reshape(blocks, block_rows, local_heads, HEAD_DIM)
    item_blocks = slot_item.reshape(blocks, block_rows)
    scale_blocks = slot_scale.reshape(blocks, block_rows)
    key_wanted = jnp.min(scale_blocks, axis=1) <= jnp.max(my_scale)

    def first_pass(running, inputs):
        key_block, item_block, scale_block, wanted = inputs

        def first_compute_block(state_now):
            scores, allowed = pair_scores(
                query_heads, key_block, my_item, item_block, my_scale, scale_block
            )
            new_peak = jnp.maximum(state_now[0], jnp.max(scores, axis=2))
            terms = jnp.where(allowed, jnp.exp(scores - new_peak[:, :, None]), 0.0)
            return (
                new_peak,
                state_now[1] * jnp.exp(state_now[0] - new_peak) + jnp.sum(terms, axis=2),
            )

        return (lax.cond(wanted, first_compute_block, lambda state_now: state_now, running), None)

    initial = (
        jnp.full((local_heads, tok_rows), -1e30, jnp.float32),
        jnp.zeros((local_heads, tok_rows), jnp.float32),
    )
    (row_peak, summed), _ = lax.scan(
        first_pass, initial, (key_blocks, item_blocks, scale_blocks, key_wanted)
    )
    log_total = row_peak + jnp.log(summed)

    def second_pass(running, inputs):
        key_block, value_block, item_block, scale_block, wanted = inputs

        def second_compute_block(total_now):
            scores, allowed = pair_scores(
                query_heads, key_block, my_item, item_block, my_scale, scale_block
            )
            rounded = jnp.where(allowed, jnp.exp(scores - log_total[:, :, None]), 0.0).astype(
                jnp.bfloat16
            )
            return total_now + jnp.einsum(
                "hqk,khd->qhd", rounded, value_block, preferred_element_type=jnp.float32
            )

        return (lax.cond(wanted, second_compute_block, lambda total_now: total_now, running), None)

    heads_out, _ = lax.scan(
        second_pass,
        jnp.zeros((tok_rows, local_heads, HEAD_DIM), jnp.float32),
        (key_blocks, value_blocks, item_blocks, scale_blocks, key_wanted),
    )
    heads_low = heads_out.reshape(tok_rows, local_width).astype(jnp.bfloat16)
    attn_out = lax.psum(
        jnp.dot(heads_low, w_out, preferred_element_type=jnp.float32).astype(jnp.bfloat16), "head"
    ).astype(jnp.float32)
    hidden = tok_float + gamma_one * attn_out
    b_pre, b_back = jax.vjp(modulate, hidden, scale_two, shift_two)
    b_low = b_pre.astype(jnp.bfloat16)
    up_proj = jnp.dot(b_low, w_fc1, preferred_element_type=jnp.float32)
    act_pre, act_back = jax.vjp(lambda values: jax.nn.gelu(values, approximate=True), up_proj)
    act_low = act_pre.astype(jnp.bfloat16)
    mlp_out = lax.psum(
        jnp.dot(act_low, w_fc2, preferred_element_type=jnp.float32).astype(jnp.bfloat16), "head"
    ).astype(jnp.float32)
    output = (hidden + gamma_two * mlp_out).astype(jnp.bfloat16)
    out_grad = cotangent.astype(jnp.float32)
    mlp_grad = (gamma_two * out_grad).astype(jnp.bfloat16)
    fc2_weight_grad = jnp.einsum("tf,td->fd", act_low, mlp_grad, preferred_element_type=jnp.float32)
    act_grad = jnp.einsum("td,fd->tf", mlp_grad, w_fc2, preferred_element_type=jnp.float32)
    up_grad = act_back(act_grad)[0].astype(jnp.bfloat16)
    fc1_weight_grad = jnp.einsum("td,tf->df", b_low, up_grad, preferred_element_type=jnp.float32)
    b_grad = lax.psum(
        jnp.einsum("tf,df->td", up_grad, w_fc1, preferred_element_type=jnp.float32).astype(
            jnp.bfloat16
        ),
        "head",
    ).astype(jnp.float32)
    hidden_part, scale_two_grad, shift_two_grad = b_back(b_grad)
    hidden_grad = out_grad + hidden_part
    attn_grad = (gamma_one * hidden_grad).astype(jnp.bfloat16)
    out_weight_grad = jnp.einsum(
        "tf,te->fe", heads_low, attn_grad, preferred_element_type=jnp.float32
    )
    grad_low = jnp.einsum("te,fe->tf", attn_grad, w_out, preferred_element_type=jnp.float32).astype(
        jnp.bfloat16
    )
    grad_heads = grad_low.reshape(tok_rows, local_heads, HEAD_DIM)
    delta = jnp.einsum("qhd,qhd->hq", grad_heads.astype(jnp.float32), heads_out)

    def step_block(running, inputs):
        key_block, value_block, item_block, scale_block, wanted = inputs

        def step_compute_block(total_now):
            scores, allowed = pair_scores(
                query_heads, key_block, my_item, item_block, my_scale, scale_block
            )
            weights = jnp.where(allowed, jnp.exp(scores - log_total[:, :, None]), 0.0)
            weight_grad = jnp.einsum(
                "qhd,khd->hqk", grad_heads, value_block, preferred_element_type=jnp.float32
            )
            score_grad = (weights * (weight_grad - delta[:, :, None])).astype(jnp.bfloat16)
            total_now = (
                total_now
                + jnp.einsum(
                    "hqk,khd->qhd", score_grad, key_block, preferred_element_type=jnp.float32
                )
                * 0.125
            )
            key_term = (
                jnp.einsum(
                    "hqk,qhd->khd", score_grad, query_heads, preferred_element_type=jnp.float32
                )
                * 0.125
            )
            value_term = jnp.einsum(
                "hqk,qhd->khd",
                weights.astype(jnp.bfloat16),
                grad_heads,
                preferred_element_type=jnp.float32,
            )
            return (total_now, (key_term, value_term))

        def skip_block(total_now):
            nothing = jnp.zeros((block_rows, local_heads, HEAD_DIM), jnp.float32)
            return (total_now, (nothing, nothing))

        return lax.cond(wanted, step_compute_block, skip_block, running)

    query_grad, (key_terms, value_terms) = lax.scan(
        step_block,
        jnp.zeros((tok_rows, local_heads, HEAD_DIM), jnp.float32),
        (key_blocks, value_blocks, item_blocks, scale_blocks, key_wanted),
    )
    key_grad, value_grad = (
        lax.psum_scatter(
            key_terms.reshape(slot_count, local_width), "tok", scatter_dimension=0, tiled=True
        ),
        lax.psum_scatter(
            value_terms.reshape(slot_count, local_width), "tok", scatter_dimension=0, tiled=True
        ),
    )
    qkv_grad = jnp.stack(
        [query_grad.reshape(tok_rows, local_width), key_grad, value_grad], axis=1
    ).astype(jnp.bfloat16)
    qkv_weight_grad = jnp.einsum("td,tce->dce", a_low, qkv_grad, preferred_element_type=jnp.float32)
    a_grad = lax.psum(
        jnp.einsum("tce,dce->td", qkv_grad, w_qkv, preferred_element_type=jnp.float32).astype(
            jnp.bfloat16
        ),
        "head",
    ).astype(jnp.float32)
    tok_part, scale_one_grad, shift_one_grad = a_back(a_grad)
    d_tokens = (hidden_grad + tok_part).astype(jnp.bfloat16)
    token_modes = jnp.stack(
        [
            hidden_grad * attn_out,
            out_grad * mlp_out,
            scale_one_grad,
            scale_two_grad,
            shift_one_grad,
            shift_two_grad,
        ],
        axis=1,
    )
    mode_part = jnp.einsum(
        "ti,tf->if", item_pick, token_modes.reshape(tok_rows, 6 * full_width), precision=HIGH
    ).reshape(item_count, 6, full_width)
    qkv_sum, out_sum, fc1_sum, fc2_sum, mode_grad = lax.psum(
        (qkv_weight_grad, out_weight_grad, fc1_weight_grad, fc2_weight_grad, mode_part), "tok"
    )
    cond_grad = jnp.zeros((item_count, full_width), jnp.float32)
    for component in range(6):
        cond_grad = cond_grad + jnp.dot(
            mode_grad[:, component], w_ada[component].astype(jnp.float32).T, precision=HIGH
        )
    pre_grad = silu_back(cond_grad)[0]
    own_pre = lax.dynamic_slice_in_dim(pre_grad, first_col, local_width, 1)
    table_grad = jnp.einsum("ic,id->cd", class_pick.astype(jnp.float32), own_pre, precision=HIGH)
    own_modes = lax.dynamic_slice_in_dim(mode_grad, first_col, local_width, 2)
    ada_grad = jnp.einsum("id,ice->cde", cond_low.astype(jnp.float32), own_modes, precision=HIGH)
    return (output, d_tokens, table_grad, ada_grad, qkv_sum, out_sum, fc1_sum, fc2_sum)


def solution(mesh):
    placed = (
        P("tok", None),
        P(),
        P(),
        P(),
        P(),
        P(),
        P(None, None, "head"),
        P("head", None),
        P(None, "head"),
        P("head", None),
        P("tok", None),
    )
    return jax.shard_map(
        on_device,
        mesh=mesh,
        in_specs=placed,
        out_specs=(
            P("tok", None),
            P("tok", None),
            P(None, "head"),
            P(None, None, "head"),
            P(None, None, "head"),
            P("head", None),
            P(None, "head"),
            P("head", None),
        ),
        check_vma=False,
    )
```

profile of v0, /device:TPU:0, one launch (start us, length us, event | category | flops | bytes accessed | tf_op | source)
XLA Modules:
  0.0 593.2 jit_solution(18391898354269014876)
XLA Ops:
  9.9 2.7 add_divide_fusion
  12.6 6.3 %convolution_bitcast_fusion.2 = f32[6,1024,3]{1,2,0:T(4,128)S(1)} fusion(bf16[6,1024,1024]{2,1,0:T(8,128)(2,1)} %param.22, f32[3,1024]{1,0:T(4,128)S(1)} %get-tuple-element.325), kind=kOutput, calls=%fused_computation.81 | convolution fusion | flops 37764096 | bytes 12668928 | tf_op jit(solution)/shard_map/id,cde->ice/dot_general | solution.py:65
  19.0 2.7 fusion.95
  21.8 2.7 copy-done.2
  30.5 23.0 %all-gather.5.cloned.1.call-done = bf16[2048,1,256]{0,2,1:T(8,128)(2,1)} async-done(((bf16[256,1,256]{0,2,1:T(8,128)(2,1)}), bf16[2048,1,256]{0,2,1:T(8,128)(2,1)}) %all-gather.5.cloned.1.call-update) | async-done | bytes 1048592 | tf_op jit(solution)/shard_map/all_gather | solution.py:89
  53.5 6.0 %conditional.3 = ((f32[4,256]{1,0:T(4,128)S(1)}, f32[4,256]{1,0:T(4,128)S(1)})) conditional(s32[]{:T(128)} %convert_element_type.108, (f32[4,256]{1,0:T(4,128)S(1)}, f32[4,256]{1,0:T(4,128)S(1)}) %tuple.59, (s32[256]{0:T(256)S(1)}, s32[2048]{0:T(1024)S(1)}, s32[2048]{0:T(1024)S(1)}, s32[256]{0:T(256)S(1)}, bf16[256,4,64]{0,2,1:T(8,128)(2,1)S(1)}, ...), branch_computations={%region_4.5_spmd, %region_5.8_spmd} | conditional | flops 286787584 | bytes 19601432 | solution.py:114
  54.0 3.0 fusion
  57.0 2.5 select_reduce_fusion
  60.2 19.4 %all-gather.7.cloned.1.call-done = bf16[2048,1,256]{0,2,1:T(8,128)(2,1)} async-done(((bf16[256,1,256]{0,2,1:T(8,128)(2,1)}), bf16[2048,1,256]{0,2,1:T(8,128)(2,1)}) %all-gather.7.cloned.1.call-update) | async-done | bytes 1048592 | tf_op jit(solution)/shard_map/all_gather | solution.py:90
  79.6 6.8 %conditional.4 = (f32[256,4,64]{0,2,1:T(8,128)S(1)}) conditional(s32[]{:T(128)} %convert_element_type.108, f32[256,4,64]{0,2,1:T(8,128)S(1)} %broadcast.241, (s32[256]{0:T(256)S(1)}, s32[2048]{0:T(1024)S(1)}, s32[2048]{0:T(1024)S(1)}, s32[256]{0:T(256)S(1)}, bf16[256,4,64]{0,2,1:T(8,128)(2,1)S(1)}, /*index=5*/bf16[2048,4,64]{0,2,1:T(8,128)(2,1)}, ...), branch_computations={%region_8.9_spmd, %region_9.10_spmd} | conditional | flops 548995072 | bytes 3823624 | solution.py:139
  81.1 5.3 fusion.3
  87.7 38.4 %all-reduce.7.cloned.1.call-done = bf16[256,1024]{1,0:T(8,128)(2,1)} async-done(((bf16[256,1024]{1,0:T(8,128)(2,1)}), bf16[256,1024]{1,0:T(8,128)(2,1)}) %all-reduce.7.cloned.1.call-update) | async-done | bytes 524304 | tf_op jit(solution)/shard_map/psum | solution.py:147
  132.2 3.1 fusion.64
  137.7 38.4 %all-reduce.9.cloned.1.call-done = bf16[256,1024]{1,0:T(8,128)(2,1)} async-done(((bf16[256,1024]{1,0:T(8,128)(2,1)}), bf16[256,1024]{1,0:T(8,128)(2,1)}) %all-reduce.9.cloned.1.call-update) | async-done | bytes 524304 | tf_op jit(solution)/shard_map/psum | solution.py:166
  183.4 16.5 %conditional.5 = (f32[256,4,64]{0,2,1:T(8,128)S(1)}, f32[2048,4,64]{0,2,1:T(8,128)}, f32[2048,4,64]{0,2,1:T(8,128)}) conditional(s32[]{:T(128)} %convert_element_type.108, f32[256,4,64]{0,2,1:T(8,128)S(1)} %broadcast.241, (s32[256]{0:T(256)}, s32[2048]{0:T(1024)}, s32[2048]{0:T(1024)}, s32[256]{0:T(256)}, bf16[256,4,64]{0,2,1:T(8,128)(2,1)S(1)}, ...), branch_computations={%region_17.18_spmd, %region_18.19_spmd.clone} | conditional | flops 1369701376 | bytes 57780444 | solution.py:221
  183.9 2.6 fusion.120
  187.1 4.6 multiply_convert_fusion
  193.2 2.2 fusion.14
  195.3 4.5 fusion.11
  199.9 2.9 copy.31
  202.9 2.9 copy.30
  205.8 3.6 convolution_convert_fusion.2
  209.4 4.4 fusion.109
  214.6 29.6 %reduce-scatter.5.cloned.1.call-done = f32[256,256]{1,0:T(8,128)} async-done(((f32[2048,256]{1,0:T(8,128)}), f32[256,256]{1,0:T(8,128)}) %reduce-scatter.5.cloned.1.call-update) | async-done | bytes 262160 | tf_op jit(solution)/shard_map/reduce_scatter | solution.py:232
  245.1 44.4 %reduce-scatter.3.cloned.1.call-done = f32[256,256]{1,0:T(8,128)} async-done(((f32[2048,256]{1,0:T(8,128)}), f32[256,256]{1,0:T(8,128)}) %reduce-scatter.3.cloned.1.call-update) | async-done | bytes 262160 | tf_op jit(solution)/shard_map/reduce_scatter | solution.py:229
  290.4 2.9 fusion.44
  293.5 3.9 fusion.123
  299.9 2.3 fusion.81
  302.2 43.5 %all-reduce.13.cloned.1.call-done = (bf16[256,1024]{1,0:T(8,128)(2,1)}, bf16[256,1024]{1,0:T(8,128)(2,1)}) async-done(((bf16[256,1024]{1,0:T(8,128)(2,1)}, bf16[256,1024]{1,0:T(8,128)(2,1)}), (bf16[256,1024]{1,0:T(8,128)(2,1)}, bf16[256,1024]{1,0:T(8,128)(2,1)})) %all-reduce.13.cloned.1.call-update) | async-done | bytes 1048592 | tf_op jit(solution)/shard_map/psum | solution.py:156
  345.7 2.4 fusion.69
  348.1 2.3 fusion.74
  350.5 2.3 fusion.71
  355.0 6.7 %copy.33 = f32[256,6,1024]{0,2,1:T(8,128)} copy(f32[256,6,1024]{2,0,1:T(8,128)} %fusion.72) | data formatting | bytes 12582912 | tf_op jit(solution)/shard_map/stack | solution.py:248
  361.7 6.3 %fusion.20 = f32[3,6,1024]{2,0,1:T(4,128)} fusion(f32[256,6,1024]{0,2,1:T(8,128)} %copy.33, s32[256]{0:T(256)S(1)} %copy-done.38), kind=kOutput, calls=%fused_computation.29 | convolution fusion | flops 56623872 | bytes 6366208 | tf_op jit(solution)/shard_map/ti,tf->if/dot_general | solution.py:259
  369.8 3.2 fusion.115
  374.0 168.6 %all-reduce.11.cloned.1.call-done = (f32[3,6,1024]{2,0,1:T(4,128)}, f32[1024,3,256]{2,0,1:T(8,128)}, f32[256,1024]{1,0:T(8,128)}, f32[1024,1024]{1,0:T(8,128)}, f32[1024,1024]{1,0:T(8,128)}) async-done(((f32[3,6,1024]{2,0,1:T(4,128)}, f32[1024,3,256]{2,0,1:T(8,128)}, f32[256,1024]{1,0:T(8,128)}, f32[1024,1024]{1,0:T(8,128)}, f32[1024,1024]{1,0:T(8,128)}), (f32[3,6,1024]{2,0,1:T(4,128)}, ...) | async-done | bytes 12656656 | tf_op jit(solution)/shard_map/psum | solution.py:262
  542.6 3.4 fusion.22
  546.0 3.3 fusion.24
  549.3 3.3 fusion.26
  552.7 3.3 fusion.28
  556.0 3.3 fusion.30
  559.3 4.6 convolution_bitcast_fusion
  563.9 6.6 %copy.35 = f32[6,1024,256]{2,1,0:T(8,128)} copy(f32[6,1024,256]{1,2,0:T(8,128)} %convolution_bitcast_fusion) | data formatting | bytes 12582912
  570.5 3.5 fusion.49
  574.0 2.4 fusion.83
  576.3 3.8 copy.74
  581.1 2.1 copy.76
  584.2 2.0 copy.77
  (178 shorter events, 41.3 us)
Async XLA Ops:
  7.2 124.3 %copy-start = (bf16[1024,1024]{1,0:T(8,128)(2,1)S(1)}, bf16[1024,1024]{1,0:T(8,128)(2,1)}, u32[]{:S(2)}) copy-start(bf16[1024,1024]{1,0:T(8,128)(2,1)} %param.25) | copy-start | bytes 6291460
  7.2 46.3 %all-gather.5.cloned.1.call-start = ((), (), s32[]{:S(2)}) async-start(), calls=%async_computation.6 | async-start | bytes 1179648 | tf_op jit(solution)/shard_map/all_gather | solution.py:89
  8.6 13.2 %copy-start.33 = (f32[256]{0:T(256)}, f32[256]{0:T(256)S(1)}, u32[]{:S(2)}) copy-start(f32[256]{0:T(256)S(1)} %broadcast_multiply_fusion.1) | copy-start | bytes 3076
  9.9 9.0 %copy-start.49 = (f32[256]{0:T(256)}, f32[256]{0:T(256)S(1)}, u32[]{:S(2)}) copy-start(f32[256]{0:T(256)S(1)} %fusion.65) | copy-start | bytes 3076
  9.9 11.8 %copy-start.47 = (f32[256]{0:T(256)}, f32[256]{0:T(256)S(1)}, u32[]{:S(2)}) copy-start(f32[256]{0:T(256)S(1)} %fusion.102) | copy-start | bytes 3076
  12.6 6.3 %copy-start.31 = (s32[2048]{0:T(1024)S(1)}, s32[2048]{0:T(1024)}, u32[]{:S(2)}) copy-start(s32[2048]{0:T(1024)} %param.19) | copy-start | bytes 24580
  18.9 5.5 copy-start.3
  18.9 6.6 %copy-start.54 = (bf16[1024,3,256]{2,0,1:T(8,128)(2,1)S(1)}, bf16[1024,3,256]{2,0,1:T(8,128)(2,1)}, u32[]{:S(2)}) copy-start(bf16[1024,3,256]{2,0,1:T(8,128)(2,1)} %param.23) | copy-start | bytes 4718596
  19.0 60.5 %copy-start.37 = (s32[256]{0:T(256)}, s32[256]{0:T(256)S(1)}, u32[]{:S(2)}) copy-start(s32[256]{0:T(256)S(1)} %dynamic_slice.43) | copy-start | bytes 3076
  19.0 8.8 %copy-start.29 = (s32[2048]{0:T(1024)S(1)}, s32[2048]{0:T(1024)}, u32[]{:S(2)}) copy-start(s32[2048]{0:T(1024)} %param.20) | copy-start | bytes 24580
  27.1 52.5 %all-gather.7.cloned.1.call-start = ((), (), s32[]{:S(2)}) async-start(), calls=%async_computation.7 | async-start | bytes 1179648 | tf_op jit(solution)/shard_map/all_gather | solution.py:90
  27.8 98.2 %all-reduce.7.cloned.1.call-start = ((), (), s32[]{:S(2)}) async-start(), calls=%async_computation.2 | async-start | bytes 1048576 | tf_op jit(solution)/shard_map/psum | solution.py:147
  29.2 50.4 %copy-start.40 = (s32[256]{0:T(256)}, s32[256]{0:T(256)S(1)}, u32[]{:S(2)}) copy-start(s32[256]{0:T(256)S(1)} %get-tuple-element.317) | copy-start | bytes 3076
  79.6 6.9 %copy-start.19 = (bf16[256,1024]{1,0:T(8,128)(2,1)S(1)}, bf16[256,1024]{1,0:T(8,128)(2,1)}, u32[]{:S(2)}) copy-start(bf16[256,1024]{1,0:T(8,128)(2,1)} %param.24) | copy-start | bytes 1572868
  87.6 88.5 %all-reduce.9.cloned.1.call-start = ((), (), s32[]{:S(2)}) async-start(), calls=%async_computation.3 | async-start | bytes 1048576 | tf_op jit(solution)/shard_map/psum | solution.py:166
  126.1 6.1 %copy-start.53 = (bf16[1024,1024]{1,0:T(8,128)(2,1)S(1)}, bf16[1024,1024]{1,0:T(8,128)(2,1)}, u32[]{:S(2)}) copy-start(bf16[1024,1024]{1,0:T(8,128)(2,1)} %param.26) | copy-start | bytes 6291460
  132.2 3.1 copy-start.9
  137.7 42.7 %copy-start.5 = (bf16[256,1024]{1,0:T(8,128)(2,1)S(1)}, bf16[256,1024]{1,0:T(8,128)(2,1)}, u32[]{:S(2)}) copy-start(bf16[256,1024]{1,0:T(8,128)(2,1)} %param.27) | copy-start | bytes 1572868
  137.7 106.5 %reduce-scatter.5.cloned.1.call-start = ((), (), s32[]{:S(2)}) async-start(), calls=%async_computation.5 | async-start | bytes 2359296 | tf_op jit(solution)/shard_map/reduce_scatter | solution.py:232
  180.3 3.1 copy-start.42
  183.9 3.2 copy-start.55
  187.1 4.6 copy-start.6
  202.8 86.7 %reduce-scatter.3.cloned.1.call-start = ((), (), s32[]{:S(2)}) async-start(), calls=%async_computation.4 | async-start | bytes 2359296 | tf_op jit(solution)/shard_map/reduce_scatter | solution.py:229
  205.8 140.0 %all-reduce.13.cloned.1.call-start = ((), (), s32[]{:S(2)}) async-start(), calls=%async_computation.9 | async-start | bytes 2097152 | tf_op jit(solution)/shard_map/psum | solution.py:156
  205.8 3.6 copy-start.10
  209.4 84.0 %copy-start.12 = (bf16[256,1024]{1,0:T(8,128)(2,1)S(1)}, bf16[256,1024]{1,0:T(8,128)(2,1)}, u32[]{:S(2)}) copy-start(bf16[256,1024]{1,0:T(8,128)(2,1)} %copy-done.11) | copy-start | bytes 1572868
  290.4 7.0 %copy-start.24 = (bf16[256,4,64]{0,2,1:T(8,128)(2,1)S(1)}, bf16[256,4,64]{0,2,1:T(8,128)(2,1)}, u32[]{:S(2)}) copy-start(bf16[256,4,64]{0,2,1:T(8,128)(2,1)} %copy-done.23) | copy-start | bytes 393220
  293.4 249.3 %all-reduce.11.cloned.1.call-start = ((), (), s32[]{:S(2)}) async-start(), calls=%async_computation.8 | async-start | bytes 25362432 | tf_op jit(solution)/shard_map/psum | solution.py:262
  293.4 4.0 copy-start.14
  293.4 5.2 copy-start.20
  293.5 5.2 copy-start.43
  293.5 6.5 %copy-start.22 = (bf16[256,1024,1]{1,0,2:T(8,128)(2,1)S(1)}, bf16[256,1024,1]{1,0,2:T(8,128)(2,1)}, u32[]{:S(2)}) copy-start(bf16[256,1024,1]{1,0,2:T(8,128)(2,1)} %copy-done.21) | copy-start | bytes 1572868
  293.5 6.5 %copy-start.27 = (bf16[256,1,256]{2,0,1:T(8,128)(2,1)S(1)}, bf16[256,1,256]{2,0,1:T(8,128)(2,1)}, u32[]{:S(2)}) copy-start(bf16[256,1,256]{2,0,1:T(8,128)(2,1)} %copy.32) | copy-start | bytes 393220
  297.4 50.7 %copy-start.4 = (bf16[256,1024]{1,0:T(8,128)(2,1)S(1)}, bf16[256,1024]{1,0:T(8,128)(2,1)}, u32[]{:S(2)}) copy-start(bf16[256,1024]{1,0:T(8,128)(2,1)} %param.17) | copy-start | bytes 1572868
  298.7 49.4 %copy-start.34 = (f32[256]{0:T(256)S(1)}, f32[256]{0:T(256)}, u32[]{:S(2)}) copy-start(f32[256]{0:T(256)} %copy-done.33) | copy-start | bytes 3076
  298.7 49.4 %copy-start.48 = (f32[256]{0:T(256)S(1)}, f32[256]{0:T(256)}, u32[]{:S(2)}) copy-start(f32[256]{0:T(256)} %copy-done.47) | copy-start | bytes 3076
  298.7 51.8 %copy-start.36 = (f32[256]{0:T(256)S(1)}, f32[256]{0:T(256)}, u32[]{:S(2)}) copy-start(f32[256]{0:T(256)} %copy-done.35) | copy-start | bytes 3076
  298.7 51.8 %copy-start.46 = (f32[256]{0:T(256)S(1)}, f32[256]{0:T(256)}, u32[]{:S(2)}) copy-start(f32[256]{0:T(256)} %copy-done.45) | copy-start | bytes 3076
  345.7 7.0 %copy-start.7 = (bf16[256,1024]{1,0:T(8,128)(2,1)S(1)}, bf16[256,1024]{1,0:T(8,128)(2,1)}, u32[]{:S(2)}) copy-start(bf16[256,1024]{1,0:T(8,128)(2,1)} %get-tuple-element.309) | copy-start | bytes 1572868
  345.7 8.1 %copy-start.8 = (bf16[256,1024]{1,0:T(8,128)(2,1)S(1)}, bf16[256,1024]{1,0:T(8,128)(2,1)}, u32[]{:S(2)}) copy-start(bf16[256,1024]{1,0:T(8,128)(2,1)} %all-reduce.9.cloned.1.call-done) | copy-start | bytes 1572868
  355.0 6.7 %copy-start.38 = (s32[256]{0:T(256)S(1)}, s32[256]{0:T(256)}, u32[]{:S(2)}) copy-start(s32[256]{0:T(256)} %copy-done.37) | copy-start | bytes 3076
  368.0 4.9 copy-start.44
  542.6 10.1 %copy-start.28 = (f32[3,6,1024]{2,0,1:T(4,128)S(1)}, f32[3,6,1024]{2,0,1:T(4,128)}, u32[]{:S(2)}) copy-start(f32[3,6,1024]{2,0,1:T(4,128)} %get-tuple-element.303) | copy-start | bytes 221188
  563.9 10.0 %copy-start.52 = (s32[3]{0:T(128)S(1)}, s32[3]{0:T(128)}, u32[]{:S(2)}) copy-start(s32[3]{0:T(128)} %param.18) | copy-start | bytes 40
  570.5 9.6 %copy-start.25 = (f32[256,1024]{1,0:T(8,128)S(1)}, f32[256,1024]{1,0:T(8,128)}, u32[]{:S(2)}) copy-start(f32[256,1024]{1,0:T(8,128)} %get-tuple-element.341) | copy-start | bytes 3145732
  570.5 10.6 %copy-start.16 = (f32[1024,1024]{1,0:T(8,128)S(1)}, f32[1024,1024]{1,0:T(8,128)}, u32[]{:S(2)}) copy-start(f32[1024,1024]{1,0:T(8,128)} %get-tuple-element.342) | copy-start | bytes 12582916
  580.1 4.1 copy-start.15
  581.1 5.1 copy-start.1
  (16 other events, 29.5 us)
Sparse Core Ops, SparseCore 0:
  27.2 26.2 all-gather.4
  55.9 23.5 all-gather.6
  87.7 38.2 all-reduce.6
  137.8 38.2 all-reduce.8
  202.9 41.1 reduce-scatter.4
  248.2 41.2 reduce-scatter.2
  293.5 52.1 all-reduce.12
  368.1 174.4 all-reduce.10
where the time goes:
time: 602 us; the launch traced here: 593 us
  waiting for transfers between devices  406 us (67%)
  matrix products  95.8 us (16%)
  other arithmetic  37.8 us (6%)
  local copies, waits for them, and re-layouts  36.4 us (6%)
  between operations  16.2 us (3%)
    psum x1, waiting for transfers between devices, on_device(): lax.psum((qkv_weight_grad, out_weight_grad, fc1_weight_grad, fc2_weight_g...  169 us
    reduce_scatter x1, waiting for transfers between devices, on_device(): lax.psum_scatter(key_terms.reshape(slot_count, local_width), 'tok', scatt...  44.4 us
    psum x1, waiting for transfers between devices, on_device(): lax.psum(jnp.dot(act_low, w_fc2, preferred_element_type=jnp.float32).asty...  43.5 us
    psum x1, waiting for transfers between devices, on_device(): lax.psum(jnp.einsum('tf,df->td', up_grad, w_fc1, preferred_element_type=j...  38.4 us
    psum x1, waiting for transfers between devices, on_device(): lax.psum(jnp.dot(heads_low, w_out, preferred_element_type=jnp.float32).as...  38.4 us
    reduce_scatter x1, waiting for transfers between devices, on_device(): lax.psum_scatter(value_terms.reshape(slot_count, local_width), 'tok', sca...  29.6 us
    all_gather x1, waiting for transfers between devices, on_device(): lax.all_gather(key_own, 'tok', axis=0, tiled=True)  23 us
    unnamed x103, local copies, waits for them, and re-layouts  22.2 us
  transfers between devices with their start and end apart: 8, of which 8 were waited for; matrix products, arithmetic and copies ran while one was open for 6% of the time, Pallas kernels for 0%

commit v1 on v0

--- a/solution.py
+++ b/solution.py
@@ -1,15 +1,926 @@
+import functools
 import math
+import types
 
 import jax
 import jax.numpy as jnp
 from jax import lax
+from jax.experimental import pallas as pl
+from jax.experimental.pallas import tpu as pltpu
 from jax.sharding import PartitionSpec as P
 
 HEAD_DIM = 64
+COMPONENTS = 6
 
 
 EPS = 1e-06
 HIGH = lax.Precision.HIGHEST
+BF = jnp.bfloat16
+F32 = jnp.float32
+MESH = pl.DeviceIdType.MESH
+BARRED = -1e30
+EIGHTH_LOG2 = 0.125 * math.log2(math.e)
+GELU_A = math.sqrt(2.0 / math.pi)
+GELU_B = 0.044715
+COPIES = 160
+VMEM_BYTES = 62 * 1024 * 1024
+ITEM_ROWS = 16
+
+
+def dot(left, right):
+    return lax.dot_general(left, right, (((1,), (0,)), ((), ())), preferred_element_type=F32)
+
+
+def dot_nt(left, right):
+    return lax.dot_general(left, right, (((1,), (1,)), ((), ())), preferred_element_type=F32)
+
+
+def dot_tn(left, right):
+    return lax.dot_general(left, right, (((0,), (0,)), ((), ())), preferred_element_type=F32)
+
+
+def turned(block):
+    return block.astype(F32).T
+
+
+def norm_rows(values):
+    shifted = values - jnp.mean(values, axis=-1, keepdims=True)
+    inverse = lax.rsqrt(jnp.mean(shifted * shifted, axis=-1, keepdims=True) + EPS)
+    return shifted * inverse, inverse
+
+
+def norm_back(grad, normed, inverse):
+    along = jnp.mean(grad * normed, axis=-1, keepdims=True)
+    return (grad - jnp.mean(grad, axis=-1, keepdims=True) - normed * along) * inverse
+
+
+class Net:
+    def __init__(self, send, arrive):
+        self.send, self.arrive = send, arrive
+        self.made, self.waited = [], []
+
+    def copy(self, source, target, device, when=None, gets=None):
+        k = len(self.made)
+        one = pltpu.make_async_remote_copy(
+            src_ref=source,
+            dst_ref=target,
+            send_sem=self.send.at[k],
+            recv_sem=self.arrive.at[k],
+            device_id=device,
+            device_id_type=MESH,
+        )
+        self.made.append((one, when, gets))
+        on_some(when, one.start)
+        return k
+
+    def arrived(self, k):
+        one, _, gets = self.made[k]
+        on_some(gets, one.wait_recv)
+        self.waited.append(k)
+
+    def finish(self):
+        for k, (one, when, _) in enumerate(self.made):
+            on_some(when, one.wait_send)
+            if k not in self.waited:
+                self.arrived(k)
+
+
+def on_some(when, act):
+    if when is None:
+        act()
+    else:
+        pl.when(when)(act)
+
+
+def block_kernel(dims, *refs):
+    rows, width, part, hidden, items, classes = dims
+    names = list(buffers(dims))
+    (
+        tok_h, cls_s, item_v, scale_v, table_h, ada_h, wq_h, wo_h, f1_h, f2_h, cot_h,
+        out_o, dtok_o, gqkv_o, gout_o, gf1_o, gf2_o, mode_o, cond_o,
+        send_sem, arrive_sem, load_sem, *scratch,
+    ) = refs
+    b = types.SimpleNamespace(**dict(zip(names, scratch, strict=True)))
+    own = rows // 4
+    half = width // 2
+    net = Net(send_sem, arrive_sem)
+    loads = []
+
+    def load(source, target):
+        one = pltpu.make_async_copy(source, target, load_sem.at[len(loads)])
+        one.start()
+        loads.append(one)
+        return one
+
+    group = lax.axis_index("tok")
+    plane = lax.axis_index("head")
+    core = lax.rem(group, 2)
+    chip = lax.div(group, 2)
+    col, line = lax.rem(chip, 2), lax.div(chip, 2)
+    chips = [chip, line * 2 + 1 - col, (1 - line) * 2 + col, 3 - chip]
+    planes = [
+        plane,
+        lax.div(plane, 2) * 2 + 1 - lax.rem(plane, 2),
+        lax.rem(plane + 2, 4),
+        3 - plane,
+    ]
+    other = 1 - core
+    inner = (plane == 1) | (plane == 2)
+    outer = (plane == 0) | (plane == 3)
+    offsets = [(dp, dz) for dz in range(4) for dp in range(4) if dp or dz]
+
+    def at(dp, dz):
+        return (chips[dp] * 2 + core, planes[dz])
+
+    mate = (chip * 2 + other, plane)
+    mine = pl.ds(pl.multiple_of(plane * own, own), own)
+
+    l_table = load(table_h, b.table)
+    l_ada = {k: load(ada_h.at[k], b.ada.at[k]) for k in (2, 4)}
+    l_tok = load(tok_h, b.tok)
+    l_wq = load(wq_h, b.wq)
+    barrier = pltpu.get_barrier_semaphore()
+    for dp, dz in offsets:
+        pl.semaphore_signal(barrier, inc=1, device_id=at(dp, dz), device_id_type=MESH)
+    pl.semaphore_signal(barrier, inc=1, device_id=mate, device_id_type=MESH)
+
+    spot = lax.rem(lax.broadcasted_iota(jnp.int32, (3 * ITEM_ROWS, rows), 0), ITEM_ROWS)
+    picks = jnp.where(spot == item_v[group], 1.0, 0.0)
+    b.pick[...] = picks.T.astype(BF)
+
+    spot = lax.broadcasted_iota(jnp.int32, (ITEM_ROWS, classes), 0)
+    label = lax.broadcasted_iota(jnp.int32, (ITEM_ROWS, classes), 1)
+    hot = jnp.zeros((ITEM_ROWS, classes), F32)
+    for i in range(items):
+        hot = jnp.where((spot == i) & (label == cls_s[i]), 1.0, hot)
+    l_table.wait()
+    cond = dot(hot.astype(BF), b.table[...])
+    b.cond[...] = cond
+    cond_low = (cond / (1.0 + jnp.exp(-cond))).astype(BF)
+
+    def make_mode(k):
+        l_ada[k].wait()
+        value = dot(cond_low, b.ada[k])
+        high = value.astype(BF)
+        rest = value - high.astype(F32)
+        middle = rest.astype(BF)
+        b.modes[k, 0:ITEM_ROWS] = high
+        b.modes[k, ITEM_ROWS : 2 * ITEM_ROWS] = middle
+        b.modes[k, 2 * ITEM_ROWS : 3 * ITEM_ROWS] = (rest - middle.astype(F32)).astype(BF)
+
+    def per_token(k, which):
+        return dot(b.pick[which], b.modes[k])
+
+    def chunks(body):
+        def step(i, carry):
+            body(pl.ds(pl.multiple_of(i * 64, 64), 64))
+            return carry
+
+        lax.fori_loop(0, rows // 64, step, 0)
+
+    make_mode(2)
+    make_mode(4)
+
+    l_tok.wait()
+
+    def first_norm(which):
+        normed, _ = norm_rows(b.tok[which].astype(F32))
+        value = (normed * (1.0 + per_token(2, which)) + per_token(4, which)).astype(BF)
+        b.a[0, which] = value[:, :half]
+        b.a[1, which] = value[:, half:]
+
+    chunks(first_norm)
+    l_wq.wait()
+    l_wo = load(wo_h, b.wo.at[plane])
+    l_ada.update({k: load(ada_h.at[k], b.ada.at[k]) for k in (0, 3, 5, 1)})
+    l_cot = load(cot_h, b.cot)
+    l_f2 = load(f2_h, b.f2)
+    l_f1 = load(f1_h, b.f1)
+    first_store = len(loads)
+    for k in range(3):
+        value = dot(b.a[0], b.wq[k, :half]) + dot(b.a[1], b.wq[k, half:])
+        value = value.T.astype(BF)
+        for h in range(4):
+            b.q_out[h, k * 64 : (k + 1) * 64] = value[h * 64 : (h + 1) * 64]
+    pl.semaphore_wait(barrier, len(offsets) + 1)
+    sent_q = [
+        net.copy(b.q_out.at[chips[dp]], b.q_in.at[chip], at(dp, 0)) for dp in (3, 1, 2)
+    ]
+    b.q_in[chip] = b.q_out[chip]
+    sent_k = [net.copy(b.q_in.at[chip, 64:192], b.k_in.at[chip], mate)]
+    b.a_all[chip, core] = b.a[core]
+    sent_a = net.copy(b.a.at[other], b.a_all.at[chip, core], mate)
+    sent_wo = [
+        net.copy(wo_h.at[chip, core], b.wo.at[plane, chip, core], at(0, dz)) for dz in (3, 2, 1)
+    ]
+
+    spot = lax.broadcasted_iota(jnp.int32, (64, rows), 0)
+    for s in range(4):
+        for k, parity in enumerate((core, other)):
+            item, scale = item_v[s * 2 + parity], scale_v[s * 2 + parity]
+            by_item = jnp.where(item != spot - 1, BARRED, 0.0)
+            by_scale = jnp.where((spot < 32) & (scale > spot - 16), BARRED, 0.0)
+            b.kt[k * 4 + s, 64:128] = jnp.where(spot < 16, by_item, by_scale).astype(BF)
+        item, scale = item_v[s * 2 + core], scale_v[s * 2 + core]
+        by_item = jnp.where(item == spot - 1, 1.0, 0.0)
+        by_scale = jnp.where((spot < 32) & (scale == spot - 16), 1.0, 0.0)
+        b.qt[s, 64:128] = jnp.where(spot < 16, by_item, by_scale).astype(BF)
+    make_mode(0)
+    make_mode(3)
+    for one, dp in zip(sent_q, (3, 1, 2), strict=True):
+        net.arrived(one)
+        sent_k.append(net.copy(b.q_in.at[chips[dp], 64:192], b.k_in.at[chips[dp]], mate))
+    sent_all = [
+        net.copy(b.a_all.at[chip, core], b.a_all.at[chip, core], at(dp, 0)) for dp in (3, 1, 2)
+    ]
+    for one in sent_wo:
+        net.arrived(one)
+    sent_wo2 = {
+        (dp, dz): net.copy(
+            b.wo.at[planes[dz], chip, core], b.wo.at[planes[dz], chip, core], at(dp, 0)
+        )
+        for dz in (1, 2, 3)
+        for dp in (3, 1, 2)
+    }
+    make_mode(5)
+    make_mode(1)
+    l_cot.wait()
+
+    def mlp_grad(which):
+        b.mg[which] = (per_token(1, which) * b.cot[which].astype(F32)).astype(BF)
+
+    chunks(mlp_grad)
+    sent_mg = net.copy(b.mg, b.mg_in, mate)
+
+    for s in range(4):
+        b.qt[s, 0:64] = b.q_in[s, 0:64]
+        b.kt[s, 0:64] = b.q_in[s, 64:128]
+        b.vt[s] = b.q_in[s, 128:192]
+    for one in sent_k:
+        net.arrived(one)
+    for s in range(4):
+        b.kt[4 + s, 0:64] = b.k_in[s, 0:64]
+        b.vt[4 + s] = b.k_in[s, 64:128]
+    for s in range(8):
+        b.ka[s] = turned(b.kt[s]).astype(BF)
+
+    sent_h = {}
+    for dp in (3, 1, 2, 0):
+        q = chips[dp]
+        queries = b.qt[q]
+        peak = None
+        for s in range(8):
+            scores = dot(b.ka[s], queries)
+            b.scores[s] = scores
+            top = jnp.max(scores, axis=0, keepdims=True)
+            peak = top if peak is None else jnp.maximum(peak, top)
+        total = jnp.zeros((1, rows), F32)
+        result = jnp.zeros((64, rows), F32)
+        for s in range(8):
+            terms = jnp.exp2((b.scores[s] - peak) * EIGHTH_LOG2)
+            total = total + jnp.sum(terms, axis=0, keepdims=True)
+            low = terms.astype(BF)
+            b.terms[q, s] = low
+            result = result + dot(b.vt[s], low)
+        share = 1.0 / total
+        b.share[q] = share
+        result = result * share
+        b.heads[q] = result
+        b.h_out[q] = result.astype(BF)
+        for dz in (3, 2, 1, 0):
+            if dp or dz:
+                sent_h[dp, dz] = net.copy(
+                    b.h_out.at[q], b.h_in.at[plane, chip], at(dp, dz)
+                )
+    b.h_in[plane, chip] = b.h_out[chip]
+
+    for s in range(8):
+        b.vn[s] = turned(b.vt[s]).astype(BF)
+    for s in range(4):
+        b.qn[s] = turned(b.qt[s])[:, 0:64].astype(BF)
+    l_f2.wait()
+    for n in range(4):
+        cols = slice(n * 256, (n + 1) * 256)
+        b.dact[:, cols] = dot_nt(b.mg[...], b.f2[cols])
+    l_wo.wait()
+    for one in sent_wo2.values():
+        net.arrived(one)
+    sent_wo3 = [
+        net.copy(b.wo.at[planes[dz], :, core], b.wo.at[planes[dz], :, core], mate)
+        for dz in (1, 2, 3)
+    ]
+
+    for dz in range(4):
+        for dp in range(4):
+            if dp or dz:
+                net.arrived(sent_h[dp, dz])
+        if dz:
+            net.arrived(sent_wo3[dz - 1])
+        left = turned(b.h_in[planes[dz]].reshape(256, rows)).astype(BF)
+        right = b.wo[planes[dz]].reshape(256, width)
+        if dz:
+            b.attn[...] += dot(left, right)
+        else:
+            b.attn[...] = dot(left, right)
+    sent_hx = net.copy(b.h_in.at[plane, pl.ds(2 * other, 2)], b.h_mate, mate)
+
+    net.arrived(sent_a)
+    sent_all += [
+        net.copy(b.a_all.at[chip, other], b.a_all.at[chip, other], at(dp, 0)) for dp in (3, 1, 2)
+    ]
+
+    def second_norm(which):
+        value = b.tok[which].astype(F32) + per_token(0, which) * b.attn[which]
+        b.hid[which] = value
+        normed, _ = norm_rows(value)
+        value = (normed * (1.0 + per_token(3, which)) + per_token(5, which)).astype(BF)
+        b.b[0, which] = value[:, :half]
+        b.b[1, which] = value[:, half:]
+
+    chunks(second_norm)
+    l_f1.wait()
+    for n in range(4):
+        cols = slice(n * 256, (n + 1) * 256)
+        up = dot(b.b[0], b.f1[:half, cols]) + dot(b.b[1], b.f1[half:, cols])
+        square = up * up
+        bent = jnp.tanh(GELU_A * up * (1.0 + GELU_B * square))
+        gate = 0.5 * (1.0 + bent)
+        slope = gate + 0.5 * up * (1.0 - bent * bent) * (GELU_A * (1.0 + 3.0 * GELU_B * square))
+        b.act[n // 2, :, (n % 2) * 256 : (n % 2 + 1) * 256] = (up * gate).astype(BF)
+        b.ug[:, cols] = (b.dact[:, cols] * slope).astype(BF)
+    for n in range(4):
+        cols = slice(n * 256, (n + 1) * 256)
+        value = dot_nt(b.ug[...], b.f1[cols])
+        b.bg_out[:, :, cols] = value.astype(BF).reshape(4, own, 256)
+    sent_bg = [
+        net.copy(b.bg_out.at[planes[dz]], b.bg_in.at[dz - 1], at(0, dz)) for dz in (3, 2, 1)
+    ]
+
+    ways = ((0, 1, 2), (1, 2, 1))
+
+    def scatter(blocks, arrived):
+        return [
+            net.copy(blocks.at[chips[which], way], arrived.at[way, n], at(first, 0))
+            for n, pick in ((1, 3), (0, None))
+            for way, first, _ in ways
+            for which in (pick or first,)
+        ]
+
+    def scatter_on(sent, blocks, arrived):
+        for one in sent:
+            net.arrived(one)
+        for way, _, then in ways:
+            total = blocks[chips[then], way].astype(F32) + arrived[way, 1].astype(F32)
+            blocks[chips[then], way] = total.astype(BF)
+        return [
+            net.copy(blocks.at[chips[then], way], arrived.at[way, 2], at(then, 0))
+            for way, _, then in ways
+        ]
+
+    def gather(sent, blocks, arrived, total, target):
+        for one in sent:
+            net.arrived(one)
+        for way, _, _ in ways:
+            total[way] = (
+                blocks[chip, way].astype(F32)
+                + arrived[way, 0].astype(F32)
+                + arrived[way, 2].astype(F32)
+            ).astype(BF)
+        load(total, target.at[core, chip])
+        net.copy(total, target.at[core, chip], mate)
+        return [
+            net.copy(total.at[way], target.at[core, chip, way], at(dp, 0))
+            for way, dp in ((0, 2), (1, 1), (0, 1), (1, 2))
+        ]
+
+    def gather_on(sent, target):
+        for one in sent[:2]:
+            net.arrived(one)
+        return [
+            net.copy(
+                target.at[core, chips[then], way], target.at[core, chips[then], way], at(first, 0)
+            )
+            for way, first, then in ways
+        ]
+
+    sent_x = [
+        net.copy(b.act.at[other], b.act_in, mate),
+        net.copy(b.b.at[other], b.b_in, mate),
+        net.copy(b.ug, b.ug_in, mate),
+    ]
+    b.left[0] = turned(b.act[core]).astype(BF)
+    net.arrived(sent_mg)
+    net.arrived(sent_x[0])
+    b.left[1] = turned(b.act_in[...]).astype(BF)
+    for n in range(4):
+        some = slice(n * 128, (n + 1) * 128)
+        value = dot(b.left[0, some], b.mg[...]) + dot(b.left[1, some], b.mg_in[...])
+        b.g2_out[n] = value.astype(BF).reshape(2, 64, width)
+    sent_g2 = scatter(b.g2_out, b.g2_in)
+    b.left[0] = turned(b.b[core]).astype(BF)
+    net.arrived(sent_x[1])
+    b.left[1] = turned(b.b_in[...]).astype(BF)
+    net.arrived(sent_x[2])
+    for n in range(4):
+        some = slice(n * 128, (n + 1) * 128)
+        value = dot(b.left[0, some], b.ug[...]) + dot(b.left[1, some], b.ug_in[...])
+        b.g1_out[n] = value.astype(BF).reshape(2, 64, width)
+    sent_g1 = scatter(b.g1_out, b.g1_in)
+    for n in range(4):
+        cols = slice(n * 256, (n + 1) * 256)
+        value = dot(b.act[0], b.f2[:half, cols]) + dot(b.act[1], b.f2[half:, cols])
+        b.mo_out[:, :, cols] = value.astype(BF).reshape(4, own, 256)
+
+    def summed(sent, kept, arrived):
+        for one in sent:
+            net.arrived(one)
+        total = kept.astype(F32)
+        for k in range(3):
+            total = total + arrived[k].astype(F32)
+        return total
+
+    def mode_sums(k, value):
+        high = value.astype(BF)
+        low = (value - high.astype(F32)).astype(BF)
+        picked = turned(b.pick[mine])[0:ITEM_ROWS].astype(BF)
+        value = (dot(picked, high) + dot(picked, low))[0:8]
+        b.ms[0, k * 8 : (k + 1) * 8] = value[:, :half]
+        b.ms[1, k * 8 : (k + 1) * 8] = value[:, half:]
+
+    def plane_scatter(blocks, arrived, far):
+        far_sent = net.copy(blocks.at[planes[3]], far, at(0, 1), outer, inner)
+        sent = [
+            net.copy(blocks.at[planes[2]], arrived.at[1], at(0, 2), outer, inner),
+            net.copy(blocks.at[planes[3]], arrived.at[2], at(0, 3), inner, inner),
+            net.copy(blocks.at[planes[1]], arrived.at[0], at(0, 1)),
+        ]
+
+        @pl.when(outer)
+        def _():
+            arrived[2] = jnp.zeros(arrived.shape[1:], BF)
+
+        return sent, far_sent
+
+    def plane_scatter_on(far_sent, blocks, arrived, far):
+        net.arrived(far_sent)
+
+        @pl.when(inner)
+        def _():
+            total = blocks[planes[2]].astype(F32) + far[...].astype(F32)
+            blocks[planes[2]] = total.astype(BF)
+
+        return net.copy(blocks.at[planes[2]], arrived.at[1], at(0, 2), inner, outer)
+
+    def plane_gather(source, target):
+        return [
+            net.copy(source, target.at[plane], at(0, 2)),
+            net.copy(source, target.at[plane], at(0, 3), inner, inner),
+            net.copy(source, target.at[plane], at(0, 1)),
+        ]
+
+    def plane_gather_on(sent, target):
+        net.arrived(sent[0])
+        return net.copy(target.at[planes[2]], target.at[planes[2]], at(0, 1), inner, outer)
+
+    b_grad = summed(sent_bg, b.bg_out[plane], b.bg_in)
+    normed, inverse = norm_rows(b.hid[mine])
+    h_grad = b.cot[mine].astype(F32) + norm_back(
+        b_grad * (1.0 + per_token(3, mine)), normed, inverse
+    )
+    b.hg[...] = h_grad
+    attn_grad = (per_token(0, mine) * h_grad).astype(BF)
+    b.ag[plane] = attn_grad
+    for n in range(4):
+        value = dot_nt(attn_grad, b.wo[n].reshape(256, width)).astype(BF)
+        for h in range(4):
+            some = value[:, h * 64 : (h + 1) * 64]
+            b.do_out[n, h] = jnp.concatenate([some[: own // 2], some[own // 2 :]], axis=1)
+    sent_do = {
+        (dp, dz): net.copy(
+            b.do_out.at[planes[dz], chips[dp]], b.do_in.at[chip, plane], at(dp, dz)
+        )
+        for dp, dz in reversed(offsets)
+    }
+    b.do_in[chip, plane] = b.do_out[plane, chip]
+    mode_sums(0, h_grad * b.attn[mine])
+    mode_sums(3, b_grad * normed)
+    mode_sums(5, b_grad)
+    sent_g2 = scatter_on(sent_g2, b.g2_out, b.g2_in)
+    sent_g1 = scatter_on(sent_g1, b.g1_out, b.g1_in)
+
+    for one in sent_do.values():
+        net.arrived(one)
+    sent_mo, far_mo = plane_scatter(b.mo_out, b.mo_in, b.mo_far)
+    sent_ag = plane_gather(b.ag.at[plane], b.ag)
+    for s in range(4):
+        for n in range(4):
+            both = b.do_in[s, n]
+            b.dn[s, n * own : n * own + own // 2] = both[:, 0:64]
+            b.dn[s, n * own + own // 2 : (n + 1) * own] = both[:, 64:128]
+        value = turned(b.dn[s])
+        b.dt[s] = value.astype(BF)
+        b.delta[s] = jnp.sum(value * b.heads[s], axis=0, keepdims=True)
+        b.dn[s] = (value * b.share[s]).T.astype(BF)
+        b.dq[s] = jnp.zeros((64, rows), F32)
+
+    def attend_back(s, carry):
+        keys, values = b.kt[s, 0:64], b.vn[s]
+        key_grad = jnp.zeros((rows, 64), F32)
+        value_grad = jnp.zeros((rows, 64), F32)
+        for q in range(4):
+            terms = b.terms[q, s]
+            pull = (dot(values, b.dt[q]) - b.delta[q]) * b.share[q]
+            low = (pull * terms.astype(F32)).astype(BF)
+            b.dq[q] += dot(keys, low)
+            key_grad = key_grad + dot(low, b.qn[q])
+            value_grad = value_grad + dot(terms, b.dn[q])
+        b.dkv[s] = jnp.concatenate([key_grad * 0.125, value_grad], axis=1).T
+        return carry
+
+    lax.fori_loop(4, 8, attend_back, 0)
+    sent_dkv = net.copy(b.dkv.at[4:8], b.dkv_in, mate)
+    sent_mo.append(plane_scatter_on(far_mo, b.mo_out, b.mo_in, b.mo_far))
+    sent_g2b = gather(sent_g2, b.g2_out, b.g2_in, b.g2, gf2_o)
+    sent_g1b = gather(sent_g1, b.g1_out, b.g1_in, b.g1, gf1_o)
+    lax.fori_loop(0, 4, attend_back, 0)
+    net.arrived(sent_dkv)
+    for s in range(4):
+        b.dx_out[s, 0:64] = (b.dq[s] * 0.125).astype(BF)
+        b.dx_out[s, 64:192] = (b.dkv[s] + b.dkv_in[s]).astype(BF)
+    sent_dx = [
+        net.copy(b.dx_out.at[chips[dp]], b.dx_in.at[chip], at(dp, 0)) for dp in (3, 1, 2)
+    ]
+    sent_dxm = net.copy(b.dx_out, b.dx_mate, mate)
+    b.dx_in[chip] = b.dx_out[chip]
+
+    sent_ag.append(plane_gather_on(sent_ag, b.ag))
+
+    for one in sent_all:
+        net.arrived(one)
+    value = jnp.zeros((192, half), F32)
+    for s in range(4):
+        value = value + dot(b.dx_out[s], b.a_all[s, core])
+    net.arrived(sent_dxm)
+    for s in range(4):
+        value = value + dot(b.dx_mate[s], b.a_all[s, other])
+    b.gq[...] = value.astype(BF)
+    for one in sent_dx:
+        net.arrived(one)
+    for k in range(3):
+        value = b.dx_in[:, k * 64 : (k + 1) * 64].reshape(256, rows)
+        b.dx[k] = turned(value).astype(BF)
+    for n in range(4):
+        cols = slice(n * 256, (n + 1) * 256)
+        value = dot_nt(b.dx[0], b.wq[0, cols])
+        value = value + dot_nt(b.dx[1], b.wq[1, cols])
+        value = value + dot_nt(b.dx[2], b.wq[2, cols])
+        b.xg_out[:, :, cols] = value.astype(BF).reshape(4, own, 256)
+    sent_xg = [
+        net.copy(b.xg_out.at[planes[dz]], b.xg_in.at[dz - 1], at(0, dz)) for dz in (3, 2, 1)
+    ]
+    sent_gq = [net.copy(b.gq, gqkv_o.at[chip, core], at(dp, 0)) for dp in (3, 1, 2)]
+    load(b.gq, gqkv_o.at[chip, core])
+    net.copy(b.gq, gqkv_o.at[chip, core], mate)
+
+    sent_g2b += gather_on(sent_g2b, gf2_o)
+    sent_g1b += gather_on(sent_g1b, gf1_o)
+
+    mlp_out = summed(sent_mo, b.mo_out[plane], b.mo_in)
+    b.out[...] = (b.hid[mine] + per_token(1, mine) * mlp_out).astype(BF)
+    sent_out = plane_gather(b.out, out_o)
+    load(b.out, out_o.at[plane])
+    mode_sums(1, b.cot[mine].astype(F32) * mlp_out)
+
+    for one in sent_ag[1:]:
+        net.arrived(one)
+    sent_agm = net.copy(b.ag, b.ag_in, mate)
+    value = dot(
+        b.h_in[plane, pl.ds(2 * core, 2)].reshape(128, rows), b.ag[...].reshape(rows, width)
+    )
+    net.arrived(sent_hx)
+    net.arrived(sent_agm)
+    value = value + dot(b.h_mate[...].reshape(128, rows), b.ag_in[...].reshape(rows, width))
+    b.go_out[...] = value.astype(BF).reshape(4, 32, width)
+    sent_go = [
+        net.copy(b.go_out.at[chips[dp]], b.go_in.at[dp - 1], at(dp, 0)) for dp in (3, 1, 2)
+    ]
+
+    plane_gather_on(sent_out, out_o)
+
+    a_grad = summed(sent_xg, b.xg_out[plane], b.xg_in)
+    normed, inverse = norm_rows(b.tok[mine].astype(F32))
+    mode_sums(2, a_grad * normed)
+    mode_sums(4, a_grad)
+    sent_ms = net.copy(b.ms.at[other], b.ms_in, mate)
+    value = b.hg[...] + norm_back(a_grad * (1.0 + per_token(2, mine)), normed, inverse)
+    b.dtok[...] = value.astype(BF)
+    net.arrived(sent_ms)
+    b.m1[...] = (b.ms[core] + b.ms_in[...]).astype(BF)
+    sent_m1 = [net.copy(b.m1, b.m1_in.at[dz - 1], at(0, dz)) for dz in (3, 2, 1)]
+    sent_dt = plane_gather(b.dtok, dtok_o)
+    load(b.dtok, dtok_o.at[plane])
+
+    b.go[...] = summed(sent_go, b.go_out[chip], b.go_in).astype(BF)
+    sent_gob = [net.copy(b.go, gout_o.at[core, chip], at(dp, 0)) for dp in (3, 1, 2)]
+    load(b.go, gout_o.at[core, chip])
+    net.copy(b.go, gout_o.at[core, chip], mate)
+    b.m2[...] = summed(sent_m1, b.m1[...], b.m1_in).astype(BF)
+    sent_m2 = [net.copy(b.m2, b.m2_in.at[dp - 1], at(dp, 0)) for dp in (3, 1, 2)]
+    b.m3[...] = summed(sent_m2, b.m2[...], b.m2_in)
+    net.copy(b.m3, mode_o.at[core], mate)
+    load(b.m3, mode_o.at[core])
+    load(b.cond, cond_o)
+    plane_gather_on(sent_dt, dtok_o)
+
+    for sent, array in ((sent_g2b, gf2_o), (sent_g1b, gf1_o)):
+        for one in sent[2:]:
+            net.arrived(one)
+        for dp in (1, 2, 3):
+            where = (core, chips[dp])
+            net.copy(array.at[where], array.at[where], mate)
+    for sent, array in ((sent_gq, gqkv_o), (sent_gob, gout_o)):
+        for one, dp in zip(sent, (3, 1, 2), strict=True):
+            net.arrived(one)
+            where = (chips[dp], core) if array is gqkv_o else (core, chips[dp])
+            net.copy(array.at[where], array.at[where], mate)
+    net.finish()
+    for one in loads[first_store:]:
+        one.wait()
+
+
+def buffers(dims):
+    rows, width, part, hidden, items, classes = dims
+    own, half = rows // 4, width // 2
+    return dict(
+        tok=((rows, width), BF),
+        cot=((rows, width), BF),
+        table=((classes, width), BF),
+        ada=((COMPONENTS, width, width), BF),
+        wq=((3, width, part), BF),
+        wo=((4, 4, 2, 32, width), BF),
+        f1=((width, hidden), BF),
+        f2=((hidden, width), BF),
+        modes=((COMPONENTS, 3 * ITEM_ROWS, width), BF),
+        pick=((rows, 3 * ITEM_ROWS), BF),
+        cond=((ITEM_ROWS, width), F32),
+        a=((2, rows, half), BF),
+        a_all=((4, 2, rows, half), BF),
+        q_out=((4, 192, rows), BF),
+        q_in=((4, 192, rows), BF),
+        k_in=((4, 128, rows), BF),
+        kt=((8, 128, rows), BF),
+        ka=((8, rows, 128), BF),
+        vt=((8, 64, rows), BF),
+        vn=((8, rows, 64), BF),
+        qt=((4, 128, rows), BF),
+        qn=((4, rows, 64), BF),
+        scores=((8, rows, rows), F32),
+        terms=((4, 8, rows, rows), BF),
+        share=((4, 1, rows), F32),
+        heads=((4, 64, rows), F32),
+        h_out=((4, 64, rows), BF),
+        h_in=((4, 4, 64, rows), BF),
+        h_mate=((2, 64, rows), BF),
+        attn=((rows, width), F32),
+        hid=((rows, width), F32),
+        b=((2, rows, half), BF),
+        b_in=((rows, half), BF),
+        act=((2, rows, half), BF),
+        act_in=((rows, half), BF),
+        mg=((rows, width), BF),
+        mg_in=((rows, width), BF),
+        ug=((rows, hidden), BF),
+        ug_in=((rows, hidden), BF),
+        dact=((rows, hidden), F32),
+        left=((2, half, rows), BF),
+        bg_out=((4, own, width), BF),
+        bg_in=((3, own, width), BF),
+        mo_out=((4, own, width), BF),
+        mo_in=((3, own, width), BF),
+        mo_far=((own, width), BF),
+        xg_out=((4, own, width), BF),
+        xg_in=((3, own, width), BF),
+        g1_out=((4, 2, 64, width), BF),
+        g1_in=((2, 3, 64, width), BF),
+        g1=((2, 64, width), BF),
+        g2_out=((4, 2, 64, width), BF),
+        g2_in=((2, 3, 64, width), BF),
+        g2=((2, 64, width), BF),
+        hg=((own, width), F32),
+        ag=((4, own, width), BF),
+        ag_in=((4, own, width), BF),
+        do_out=((4, 4, own // 2, 128), BF),
+        do_in=((4, 4, own // 2, 128), BF),
+        dn=((4, rows, 64), BF),
+        dt=((4, 64, rows), BF),
+        delta=((4, 1, rows), F32),
+        dq=((4, 64, rows), F32),
+        dkv=((8, 128, rows), F32),
+        dkv_in=((4, 128, rows), F32),
+        dx_out=((4, 192, rows), BF),
+        dx_mate=((4, 192, rows), BF),
+        dx_in=((4, 192, rows), BF),
+        dx=((3, rows, part), BF),
+        gq=((192, half), BF),
+        out=((own, width), BF),
+        dtok=((own, width), BF),
+        go_out=((4, 32, width), BF),
+        go_in=((3, 32, width), BF),
+        go=((32, width), BF),
+        ms=((2, 48, half), F32),
+        ms_in=((48, half), F32),
+        m1=((48, half), BF),
+        m1_in=((3, 48, half), BF),
+        m2=((48, half), BF),
+        m2_in=((3, 48, half), BF),
+        m3=((48, half), F32),
+    )
+
+
+def finish_kernel(
+    cls_s, ada_h, out_i, dtok_i, gqkv_i, gout_i, gf1_i, gf2_i, mode_i, cond_i,
+    out_o, dtok_o, table_o, ada_o, qkv_o, wout_o, f1_o, f2_o, ada_v, sems,
+):
+    step, last = pl.program_id(0), pl.num_programs(0) - 1
+    plane = lax.axis_index("head")
+    part = table_o.shape[1]
+    mine = pl.ds(pl.multiple_of(plane * part, part), part)
+    fetch = [
+        pltpu.make_async_copy(ada_h.at[k, mine], ada_v.at[k], sems.at[k]) for k in range(COMPONENTS)
+    ]
+
+    @pl.when(step == 0)
+    def _():
+        for one in fetch:
+            one.start()
+
+    out_o[...] = out_i[0]
+    dtok_o[...] = dtok_i[0]
+    wout_o[...] = gout_i[0, 0].astype(F32)
+    f1_o[...] = gf1_i[0, 0].astype(F32).reshape(f1_o.shape)
+    f2_o[...] = gf2_i[0, 0].astype(F32).reshape(f2_o.shape)
+    for k in range(3):
+        value = gqkv_i[:, 0, k * 64 : (k + 1) * 64].astype(F32).reshape(part, 128)
+        qkv_o[k] = value.T
+    cond = cond_i[:, pl.ds(pl.multiple_of(step * 128, 128), 128)]
+    cond_low = (cond / (1.0 + jnp.exp(-cond)))[0:8]
+    low = jnp.concatenate([cond_low, cond_low], axis=0).astype(BF)
+    side = pl.ds(pl.multiple_of(lax.rem(plane, 2) * part, part), part)
+    for k in range(COMPONENTS):
+        value = mode_i[lax.div(plane, 2), k * 8 : (k + 1) * 8, side]
+        high = value.astype(BF).astype(F32)
+        both = jnp.concatenate([high, value - high], axis=0).astype(BF)
+        ada_o[k] = dot_tn(low, both)
+
+    @pl.when(step == last)
+    def _():
+        cond_grad = jnp.zeros((16, part), F32)
+        half = mode_i.shape[2]
+        for k in range(COMPONENTS):
+            fetch[k].wait()
+            for n in range(2):
+                value = mode_i[n, k * 8 : (k + 1) * 8]
+                high = value.astype(BF).astype(F32)
+                both = jnp.concatenate([high, value - high], axis=0).astype(BF)
+                cond_grad = cond_grad + dot_nt(both, ada_v[k, :, n * half : (n + 1) * half])
+        own = cond_i[0:8, mine]
+        gate = 1.0 / (1.0 + jnp.exp(-own))
+        grad = (cond_grad[0:8] + cond_grad[8:16]) * gate * (1.0 + own * (1.0 - gate))
+        spot = lax.broadcasted_iota(jnp.int32, table_o.shape, 0)
+        total = jnp.zeros(table_o.shape, F32)
+        for i in range(cls_s.shape[0]):
+            total = total + jnp.where(spot == cls_s[i], grad[i : i + 1], 0.0)
+        table_o[...] = total
+
+
+def finish(
+    class_ids, w_ada, output, d_tokens, qkv_sum, out_sum, fc1_sum, fc2_sum, mode_grad, cond, classes
+):
+    steps = 8
+    own, width = output.shape[1:]
+    half, part, hidden = width // 2, width // 4, steps * 128
+    rows = own * 4
+    anywhere = pl.BlockSpec(memory_space=pl.ANY)
+    smem = pl.BlockSpec(memory_space=pltpu.SMEM)
+    few = pl.BlockSpec((1, own // 2, width), lambda i: (i // 2, i % 2, 0))
+    table, ada, qkv, out, fc1, fc2 = (
+        (classes, part),
+        (COMPONENTS, width, part),
+        (3, width, part),
+        (part, width),
+        (width, hidden),
+        (hidden, width),
+    )
+    output, d_tokens, table, ada, qkv, out, fc1, fc2 = pl.pallas_call(
+        finish_kernel,
+        grid=(steps,),
+        out_shape=[
+            jax.ShapeDtypeStruct((rows, width), BF),
+            jax.ShapeDtypeStruct((rows, width), BF),
+        ]
+        + [jax.ShapeDtypeStruct(shape, F32) for shape in (table, ada, qkv, out, fc1, fc2)],
+        in_specs=[
+            smem,
+            anywhere,
+            few,
+            few,
+            pl.BlockSpec((4, 1, 192, half // 4), lambda i: (0, i // 4, 0, i % 4)),
+            pl.BlockSpec((1, 1, 32, width), lambda i: (i // 4, i % 4, 0, 0)),
+            pl.BlockSpec((1, 1, 2, 64, hidden), lambda i: (i // 4, i % 4, 0, 0, 0)),
+            pl.BlockSpec((1, 1, 2, 64, width), lambda i: (i // 4, i % 4, 0, 0, 0)),
+            pl.BlockSpec((2, 48, half), lambda i: (0, 0, 0)),
+            pl.BlockSpec((ITEM_ROWS, width), lambda i: (0, 0)),
+        ],
+        out_specs=[
+            pl.BlockSpec((rows // steps, width), lambda i: (i, 0)),
+            pl.BlockSpec((rows // steps, width), lambda i: (i, 0)),
+            pl.BlockSpec((classes, part), lambda i: (0, 0)),
+            pl.BlockSpec((COMPONENTS, 128, part), lambda i: (0, i, 0)),
+            pl.BlockSpec((3, 128, part), lambda i: (0, i, 0)),
+            pl.BlockSpec((32, width), lambda i: (i, 0)),
+            pl.BlockSpec((128, hidden), lambda i: (i, 0)),
+            pl.BlockSpec((128, width), lambda i: (i, 0)),
+        ],
+        scratch_shapes=[
+            pltpu.VMEM((COMPONENTS, part, width), BF),
+            pltpu.SemaphoreType.DMA((COMPONENTS,)),
+        ],
+        compiler_params=pltpu.CompilerParams(vmem_limit_bytes=VMEM_BYTES),
+    )(
+        class_ids, w_ada, output, d_tokens, qkv_sum, out_sum, fc1_sum, fc2_sum, mode_grad, cond
+    )
+    return output, d_tokens, table, ada, qkv.transpose(1, 0, 2), out, fc1, fc2
+
+
+def on_block(
+    tokens,
+    class_ids,
+    slot_item,
+    slot_scale,
+    class_table,
+    w_ada,
+    w_qkv,
+    w_out,
+    w_fc1,
+    w_fc2,
+    cotangent,
+):
+    rows, width = tokens.shape
+    part, hidden = w_qkv.shape[2], w_fc1.shape[1]
+    items, classes = class_ids.shape[0], class_table.shape[0]
+    own, half = rows // 4, width // 2
+    dims = (rows, width, part, hidden, items, classes)
+    scratch = [pltpu.VMEM(shape, dtype) for shape, dtype in buffers(dims).values()]
+    anywhere = pl.BlockSpec(memory_space=pl.ANY)
+    vmem = pl.BlockSpec(memory_space=pltpu.VMEM)
+    smem = pl.BlockSpec(memory_space=pltpu.SMEM)
+    output, d_tokens, qkv_sum, out_sum, fc1_sum, fc2_sum, mode_grad, cond = pl.pallas_call(
+        functools.partial(block_kernel, dims),
+        out_shape=[
+            jax.ShapeDtypeStruct((4, own, width), BF),
+            jax.ShapeDtypeStruct((4, own, width), BF),
+            jax.ShapeDtypeStruct((4, 2, 192, half), BF),
+            jax.ShapeDtypeStruct((2, 4, 32, width), BF),
+            jax.ShapeDtypeStruct((2, 4, 2, 64, width), BF),
+            jax.ShapeDtypeStruct((2, 4, 2, 64, width), BF),
+            jax.ShapeDtypeStruct((2, 48, half), F32),
+            jax.ShapeDtypeStruct((ITEM_ROWS, width), F32),
+        ],
+        in_specs=[anywhere, smem, vmem, vmem] + [anywhere] * 7,
+        out_specs=[anywhere] * 8,
+        scratch_shapes=[
+            pltpu.SemaphoreType.DMA((COPIES,)),
+            pltpu.SemaphoreType.DMA((COPIES,)),
+            pltpu.SemaphoreType.DMA((32,)),
+            *scratch,
+        ],
+        compiler_params=pltpu.CompilerParams(
+            collective_id=0, has_side_effects=True, vmem_limit_bytes=VMEM_BYTES
+        ),
+        cost_estimate=pl.CostEstimate(
+            flops=10_000_000_000, bytes_accessed=40_000_000, transcendentals=3_000_000
+        ),
+    )(
+        tokens,
+        class_ids,
+        slot_item.reshape(8, 1, rows),
+        slot_scale.reshape(8, 1, rows),
+        class_table,
+        w_ada,
+        w_qkv.transpose(1, 0, 2),
+        w_out.reshape(4, 2, 32, width),
+        w_fc1,
+        w_fc2,
+        cotangent,
+    )
+    return finish(
+        class_ids, w_ada, output, d_tokens, qkv_sum, out_sum, fc1_sum, fc2_sum, mode_grad, cond,
+        classes,
+    )
+
+
+def fits(mesh):
+    return mesh.shape["tok"] == 8 and mesh.shape["head"] == 4
 
 
 def layer_norm(values):
@@ -290,7 +1201,7 @@
         P("tok", None),
     )
     return jax.shard_map(
-        on_device,
+        on_block if fits(mesh) else on_device,
         mesh=mesh,
         in_specs=placed,
         out_specs=(

time: 602 us -> 152 us (0.25); the launches traced: 593 us -> 152 us
  waiting for transfers between devices: 406 us -> 0 us
  Pallas kernels: 0 us -> 151 us
  matrix products: 95.8 us -> 0 us
  other arithmetic: 37.8 us -> 0 us
  local copies, waits for them, and re-layouts: 36.4 us -> 0 us
  between operations: 16.2 us -> 0.8 us
    psum x4 -> x0, waiting for transfers between devices: 289 us -> none  [the longest x1 169 us: on_device(): lax.psum((qkv_weight_grad, out_weight_grad, fc1_weight_grad, fc2_weight_g...]
    pallas_call x0 -> x2, Pallas kernels: none -> 151 us  [the longest x1 135 us: on_block(): pl.pallas_call(functools.partial(block_kernel, dims), out_shape=[jax.Shap...]
    dot_general x31 -> x0, matrix products: 95.8 us -> none  [the longest x6 20.2 us: on_device(): jnp.dot(mode_grad[:, component], w_ada[component].astype(jnp.float32).T,...]
    reduce_scatter x2 -> x0, waiting for transfers between devices: 73.9 us -> none  [the longest x1 44.4 us: on_device(): lax.psum_scatter(key_terms.reshape(slot_count, local_width), 'tok', scatt...]
    all_gather x2 -> x0, waiting for transfers between devices: 42.3 us -> none  [the longest x1 23 us: on_device(): lax.all_gather(key_own, 'tok', axis=0, tiled=True)]
    unnamed x103 -> x0, local copies, waits for them, and re-layouts: 22.2 us -> none
    reduce_sum x9 -> x0, other arithmetic: 15.7 us -> none  [the longest x2 4.97 us: layer_norm(): shifted = values - centre]
    unnamed x6 -> x0, other arithmetic: 9.31 us -> none
  transfers between devices with their start and end apart: 8 -> 0, of which waited for: 8 -> 0; matrix products, arithmetic and copies ran while one was open for 6% -> 0% of each run, Pallas kernels for 0% -> 0%
where the time goes in v1:
time: 152 us
  Pallas kernels  151 us (99%)
    pallas_call x1, Pallas kernels, on_block(): pl.pallas_call(functools.partial(block_kernel, dims), out_shape=[jax.Shap...  135 us
    pallas_call x1, Pallas kernels, finish(): pl.pallas_call(finish_kernel, grid=(steps,), out_shape=[jax.ShapeDtypeStr...  16.3 us

profile of v1, /device:TPU:0, one launch (start us, length us, event | category | flops | bytes accessed | tf_op | source)
XLA Modules:
  0.0 151.9 jit_solution(5518483913116663598)
XLA Ops:
  0.6 134.9 %shard_map.170 = (bf16[4,64,1024]{2,1,0:T(8,128)(2,1)}, bf16[4,64,1024]{2,1,0:T(8,128)(2,1)}, bf16[4,2,192,512]{3,2,1,0:T(8,128)(2,1)}, bf16[2,4,32,1024]{3,2,1,...) custom-call(bf16[256,1024]{1,0:T(8,128)(2,1)} %refs_0_.1, ...), custom_call_target="tpu_custom_call" | custom-call | flops 10000000000 | bytes 40000000 | tf_op jit(solution)/shard_map/pallas_call | solution.py:877
  135.5 16.3 %shard_map.171 = (bf16[256,1024]{1,0:T(8,128)(2,1)}, bf16[256,1024]{1,0:T(8,128)(2,1)}, f32[1000,256]{1,0:T(8,128)}, f32[6,1024,256]{2,1,0:T(8,128)}, f32[3,1024...) custom-call(s32[3]{0:T(128)} %cls_s.1, bf16[6,1024,1024]{2,1,0:T(8,128)(2,1)} %ada_h.1, ...), custom_call_target="tpu_custom_call" | custom-call | tf_op jit(solution)/shard_map/pallas_call | solution.py:814

commit v2 on v1

--- a/solution.py
+++ b/solution.py
@@ -208,8 +208,7 @@
     ]
     b.q_in[chip] = b.q_out[chip]
     sent_k = [net.copy(b.q_in.at[chip, 64:192], b.k_in.at[chip], mate)]
-    b.a_all[chip, core] = b.a[core]
-    sent_a = net.copy(b.a.at[other], b.a_all.at[chip, core], mate)
+    sent_a = net.copy(b.a.at[other], b.a_in, mate)
     sent_wo = [
         net.copy(wo_h.at[chip, core], b.wo.at[plane, chip, core], at(0, dz)) for dz in (3, 2, 1)
     ]
@@ -230,9 +229,6 @@
     for one, dp in zip(sent_q, (3, 1, 2), strict=True):
         net.arrived(one)
         sent_k.append(net.copy(b.q_in.at[chips[dp], 64:192], b.k_in.at[chips[dp]], mate))
-    sent_all = [
-        net.copy(b.a_all.at[chip, core], b.a_all.at[chip, core], at(dp, 0)) for dp in (3, 1, 2)
-    ]
     for one in sent_wo:
         net.arrived(one)
     sent_wo2 = {
@@ -324,10 +320,6 @@
             b.attn[...] = dot(left, right)
     sent_hx = net.copy(b.h_in.at[plane, pl.ds(2 * other, 2)], b.h_mate, mate)
 
-    net.arrived(sent_a)
-    sent_all += [
-        net.copy(b.a_all.at[chip, other], b.a_all.at[chip, other], at(dp, 0)) for dp in (3, 1, 2)
-    ]
 
     def second_norm(which):
         value = b.tok[which].astype(F32) + per_token(0, which) * b.attn[which]
@@ -550,22 +542,12 @@
     sent_dx = [
         net.copy(b.dx_out.at[chips[dp]], b.dx_in.at[chip], at(dp, 0)) for dp in (3, 1, 2)
     ]
-    sent_dxm = net.copy(b.dx_out, b.dx_mate, mate)
     b.dx_in[chip] = b.dx_out[chip]
-
     sent_ag.append(plane_gather_on(sent_ag, b.ag))
 
-    for one in sent_all:
-        net.arrived(one)
-    value = jnp.zeros((192, half), F32)
-    for s in range(4):
-        value = value + dot(b.dx_out[s], b.a_all[s, core])
-    net.arrived(sent_dxm)
-    for s in range(4):
-        value = value + dot(b.dx_mate[s], b.a_all[s, other])
-    b.gq[...] = value.astype(BF)
     for one in sent_dx:
         net.arrived(one)
+    sent_dxm = net.copy(b.dx_in, b.dx_mate, mate)
     for k in range(3):
         value = b.dx_in[:, k * 64 : (k + 1) * 64].reshape(256, rows)
         b.dx[k] = turned(value).astype(BF)
@@ -578,9 +560,13 @@
     sent_xg = [
         net.copy(b.xg_out.at[planes[dz]], b.xg_in.at[dz - 1], at(0, dz)) for dz in (3, 2, 1)
     ]
-    sent_gq = [net.copy(b.gq, gqkv_o.at[chip, core], at(dp, 0)) for dp in (3, 1, 2)]
-    load(b.gq, gqkv_o.at[chip, core])
-    net.copy(b.gq, gqkv_o.at[chip, core], mate)
+
+    net.arrived(sent_a)
+    net.arrived(sent_dxm)
+    for h in range(4):
+        value = dot(b.dx_in[h], b.a[core]) + dot(b.dx_mate[h], b.a_in[...])
+        b.gq_out[h] = value.astype(BF).reshape(2, 96, half)
+    sent_gq = scatter(b.gq_out, b.gq_in)
 
     sent_g2b += gather_on(sent_g2b, gf2_o)
     sent_g1b += gather_on(sent_g1b, gf1_o)
@@ -606,6 +592,7 @@
     ]
 
     plane_gather_on(sent_out, out_o)
+    sent_gq = scatter_on(sent_gq, b.gq_out, b.gq_in)
 
     a_grad = summed(sent_xg, b.xg_out[plane], b.xg_in)
     normed, inverse = norm_rows(b.tok[mine].astype(F32))
@@ -620,6 +607,7 @@
     sent_dt = plane_gather(b.dtok, dtok_o)
     load(b.dtok, dtok_o.at[plane])
 
+    sent_gqb = gather(sent_gq, b.gq_out, b.gq_in, b.gq, gqkv_o)
     b.go[...] = summed(sent_go, b.go_out[chip], b.go_in).astype(BF)
     sent_gob = [net.copy(b.go, gout_o.at[core, chip], at(dp, 0)) for dp in (3, 1, 2)]
     load(b.go, gout_o.at[core, chip])
@@ -630,19 +618,19 @@
     net.copy(b.m3, mode_o.at[core], mate)
     load(b.m3, mode_o.at[core])
     load(b.cond, cond_o)
+    sent_gqb += gather_on(sent_gqb, gqkv_o)
     plane_gather_on(sent_dt, dtok_o)
 
-    for sent, array in ((sent_g2b, gf2_o), (sent_g1b, gf1_o)):
+    for sent, array in ((sent_g2b, gf2_o), (sent_g1b, gf1_o), (sent_gqb, gqkv_o)):
         for one in sent[2:]:
             net.arrived(one)
         for dp in (1, 2, 3):
             where = (core, chips[dp])
             net.copy(array.at[where], array.at[where], mate)
-    for sent, array in ((sent_gq, gqkv_o), (sent_gob, gout_o)):
-        for one, dp in zip(sent, (3, 1, 2), strict=True):
-            net.arrived(one)
-            where = (chips[dp], core) if array is gqkv_o else (core, chips[dp])
-            net.copy(array.at[where], array.at[where], mate)
+    for one, dp in zip(sent_gob, (3, 1, 2), strict=True):
+        net.arrived(one)
+        where = (core, chips[dp])
+        net.copy(gout_o.at[where], gout_o.at[where], mate)
     net.finish()
     for one in loads[first_store:]:
         one.wait()
@@ -664,7 +652,7 @@
         pick=((rows, 3 * ITEM_ROWS), BF),
         cond=((ITEM_ROWS, width), F32),
         a=((2, rows, half), BF),
-        a_all=((4, 2, rows, half), BF),
+        a_in=((rows, half), BF),
         q_out=((4, 192, rows), BF),
         q_in=((4, 192, rows), BF),
         k_in=((4, 128, rows), BF),
@@ -721,7 +709,9 @@
         dx_mate=((4, 192, rows), BF),
         dx_in=((4, 192, rows), BF),
         dx=((3, rows, part), BF),
-        gq=((192, half), BF),
+        gq_out=((4, 2, 96, half), BF),
+        gq_in=((2, 3, 96, half), BF),
+        gq=((2, 96, half), BF),
         out=((own, width), BF),
         dtok=((own, width), BF),
         go_out=((4, 32, width), BF),
@@ -759,9 +749,9 @@
     wout_o[...] = gout_i[0, 0].astype(F32)
     f1_o[...] = gf1_i[0, 0].astype(F32).reshape(f1_o.shape)
     f2_o[...] = gf2_i[0, 0].astype(F32).reshape(f2_o.shape)
+    sums = gqkv_i[0].astype(F32).reshape(4, 192, 128)
     for k in range(3):
-        value = gqkv_i[:, 0, k * 64 : (k + 1) * 64].astype(F32).reshape(part, 128)
-        qkv_o[k] = value.T
+        qkv_o[k] = sums[:, k * 64 : (k + 1) * 64].reshape(part, 128).T
     cond = cond_i[:, pl.ds(pl.multiple_of(step * 128, 128), 128)]
     cond_low = (cond / (1.0 + jnp.exp(-cond)))[0:8]
     low = jnp.concatenate([cond_low, cond_low], axis=0).astype(BF)
@@ -824,7 +814,7 @@
             anywhere,
             few,
             few,
-            pl.BlockSpec((4, 1, 192, half // 4), lambda i: (0, i // 4, 0, i % 4)),
+            pl.BlockSpec((1, 4, 2, 96, half // 4), lambda i: (i // 4, 0, 0, 0, i % 4)),
             pl.BlockSpec((1, 1, 32, width), lambda i: (i // 4, i % 4, 0, 0)),
             pl.BlockSpec((1, 1, 2, 64, hidden), lambda i: (i // 4, i % 4, 0, 0, 0)),
             pl.BlockSpec((1, 1, 2, 64, width), lambda i: (i // 4, i % 4, 0, 0, 0)),
@@ -879,7 +869,7 @@
         out_shape=[
             jax.ShapeDtypeStruct((4, own, width), BF),
             jax.ShapeDtypeStruct((4, own, width), BF),
-            jax.ShapeDtypeStruct((4, 2, 192, half), BF),
+            jax.ShapeDtypeStruct((2, 4, 2, 96, half), BF),
             jax.ShapeDtypeStruct((2, 4, 32, width), BF),
             jax.ShapeDtypeStruct((2, 4, 2, 64, width), BF),
             jax.ShapeDtypeStruct((2, 4, 2, 64, width), BF),

time: 152 us -> 137 us (0.901)
  Pallas kernels: 151 us -> 136 us
    pallas_call x1, Pallas kernels: 135 us -> 120 us  [on_block(): pl.pallas_call(functools.partial(block_kernel, dims), out_shape=[jax.Shap...]
where the time goes in v2:
time: 137 us
  Pallas kernels  136 us (99%)
    pallas_call x1, Pallas kernels, on_block(): pl.pallas_call(functools.partial(block_kernel, dims), out_shape=[jax.Shap...  120 us
    pallas_call x1, Pallas kernels, finish(): pl.pallas_call(finish_kernel, grid=(steps,), out_shape=[jax.ShapeDtypeStr...  16.3 us

profile of v2, /device:TPU:0, one launch (start us, length us, event | category | flops | bytes accessed | tf_op | source)
XLA Modules:
  0.0 137.1 jit_solution(1740030027336612897)
XLA Ops:
  0.6 120.0 %shard_map.170 = (bf16[4,64,1024]{2,1,0:T(8,128)(2,1)}, bf16[4,64,1024]{2,1,0:T(8,128)(2,1)}, bf16[2,4,2,96,512]{4,3,2,1,0:T(8,128)(2,1)}, bf16[2,4,32,1024]{3,2...) custom-call(bf16[256,1024]{1,0:T(8,128)(2,1)} %refs_0_.1, ...), custom_call_target="tpu_custom_call" | custom-call | flops 10000000000 | bytes 40000000 | tf_op jit(solution)/shard_map/pallas_call | solution.py:867
  120.6 16.3 %shard_map.171 = (bf16[256,1024]{1,0:T(8,128)(2,1)}, bf16[256,1024]{1,0:T(8,128)(2,1)}, f32[1000,256]{1,0:T(8,128)}, f32[6,1024,256]{2,1,0:T(8,128)}, f32[3,1024...) custom-call(s32[3]{0:T(128)} %cls_s.1, bf16[6,1024,1024]{2,1,0:T(8,128)(2,1)} %ada_h.1, ...), custom_call_target="tpu_custom_call" | custom-call | tf_op jit(solution)/shard_map/pallas_call | solution.py:804

commit v3 on v2

--- a/solution.py
+++ b/solution.py
@@ -22,7 +22,8 @@
 EIGHTH_LOG2 = 0.125 * math.log2(math.e)
 GELU_A = math.sqrt(2.0 / math.pi)
 GELU_B = 0.044715
-COPIES = 160
+COPIES = 164
+LOADS = 22
 VMEM_BYTES = 62 * 1024 * 1024
 ITEM_ROWS = 16
 
@@ -97,7 +98,7 @@
     names = list(buffers(dims))
     (
         tok_h, cls_s, item_v, scale_v, table_h, ada_h, wq_h, wo_h, f1_h, f2_h, cot_h,
-        out_o, dtok_o, gqkv_o, gout_o, gf1_o, gf2_o, mode_o, cond_o,
+        out_o, dtok_o, gqkv_o, gout_o, gf1_o, gf2_o, mode_o, cond_o, cg_o,
         send_sem, arrive_sem, load_sem, *scratch,
     ) = refs
     b = types.SimpleNamespace(**dict(zip(names, scratch, strict=True)))
@@ -135,218 +136,13 @@
     mate = (chip * 2 + other, plane)
     mine = pl.ds(pl.multiple_of(plane * own, own), own)
 
-    l_table = load(table_h, b.table)
-    l_ada = {k: load(ada_h.at[k], b.ada.at[k]) for k in (2, 4)}
-    l_tok = load(tok_h, b.tok)
-    l_wq = load(wq_h, b.wq)
-    barrier = pltpu.get_barrier_semaphore()
-    for dp, dz in offsets:
-        pl.semaphore_signal(barrier, inc=1, device_id=at(dp, dz), device_id_type=MESH)
-    pl.semaphore_signal(barrier, inc=1, device_id=mate, device_id_type=MESH)
-
-    spot = lax.rem(lax.broadcasted_iota(jnp.int32, (3 * ITEM_ROWS, rows), 0), ITEM_ROWS)
-    picks = jnp.where(spot == item_v[group], 1.0, 0.0)
-    b.pick[...] = picks.T.astype(BF)
-
-    spot = lax.broadcasted_iota(jnp.int32, (ITEM_ROWS, classes), 0)
-    label = lax.broadcasted_iota(jnp.int32, (ITEM_ROWS, classes), 1)
-    hot = jnp.zeros((ITEM_ROWS, classes), F32)
-    for i in range(items):
-        hot = jnp.where((spot == i) & (label == cls_s[i]), 1.0, hot)
-    l_table.wait()
-    cond = dot(hot.astype(BF), b.table[...])
-    b.cond[...] = cond
-    cond_low = (cond / (1.0 + jnp.exp(-cond))).astype(BF)
-
-    def make_mode(k):
-        l_ada[k].wait()
-        value = dot(cond_low, b.ada[k])
-        high = value.astype(BF)
-        rest = value - high.astype(F32)
-        middle = rest.astype(BF)
-        b.modes[k, 0:ITEM_ROWS] = high
-        b.modes[k, ITEM_ROWS : 2 * ITEM_ROWS] = middle
-        b.modes[k, 2 * ITEM_ROWS : 3 * ITEM_ROWS] = (rest - middle.astype(F32)).astype(BF)
-
-    def per_token(k, which):
-        return dot(b.pick[which], b.modes[k])
-
-    def chunks(body):
-        def step(i, carry):
-            body(pl.ds(pl.multiple_of(i * 64, 64), 64))
-            return carry
-
-        lax.fori_loop(0, rows // 64, step, 0)
-
-    make_mode(2)
-    make_mode(4)
-
-    l_tok.wait()
-
-    def first_norm(which):
-        normed, _ = norm_rows(b.tok[which].astype(F32))
-        value = (normed * (1.0 + per_token(2, which)) + per_token(4, which)).astype(BF)
-        b.a[0, which] = value[:, :half]
-        b.a[1, which] = value[:, half:]
-
-    chunks(first_norm)
-    l_wq.wait()
-    l_wo = load(wo_h, b.wo.at[plane])
-    l_ada.update({k: load(ada_h.at[k], b.ada.at[k]) for k in (0, 3, 5, 1)})
-    l_cot = load(cot_h, b.cot)
-    l_f2 = load(f2_h, b.f2)
-    l_f1 = load(f1_h, b.f1)
-    first_store = len(loads)
-    for k in range(3):
-        value = dot(b.a[0], b.wq[k, :half]) + dot(b.a[1], b.wq[k, half:])
-        value = value.T.astype(BF)
-        for h in range(4):
-            b.q_out[h, k * 64 : (k + 1) * 64] = value[h * 64 : (h + 1) * 64]
-    pl.semaphore_wait(barrier, len(offsets) + 1)
-    sent_q = [
-        net.copy(b.q_out.at[chips[dp]], b.q_in.at[chip], at(dp, 0)) for dp in (3, 1, 2)
-    ]
-    b.q_in[chip] = b.q_out[chip]
-    sent_k = [net.copy(b.q_in.at[chip, 64:192], b.k_in.at[chip], mate)]
-    sent_a = net.copy(b.a.at[other], b.a_in, mate)
-    sent_wo = [
-        net.copy(wo_h.at[chip, core], b.wo.at[plane, chip, core], at(0, dz)) for dz in (3, 2, 1)
-    ]
-
-    spot = lax.broadcasted_iota(jnp.int32, (64, rows), 0)
-    for s in range(4):
-        for k, parity in enumerate((core, other)):
-            item, scale = item_v[s * 2 + parity], scale_v[s * 2 + parity]
-            by_item = jnp.where(item != spot - 1, BARRED, 0.0)
-            by_scale = jnp.where((spot < 32) & (scale > spot - 16), BARRED, 0.0)
-            b.kt[k * 4 + s, 64:128] = jnp.where(spot < 16, by_item, by_scale).astype(BF)
-        item, scale = item_v[s * 2 + core], scale_v[s * 2 + core]
-        by_item = jnp.where(item == spot - 1, 1.0, 0.0)
-        by_scale = jnp.where((spot < 32) & (scale == spot - 16), 1.0, 0.0)
-        b.qt[s, 64:128] = jnp.where(spot < 16, by_item, by_scale).astype(BF)
-    make_mode(0)
-    make_mode(3)
-    for one, dp in zip(sent_q, (3, 1, 2), strict=True):
-        net.arrived(one)
-        sent_k.append(net.copy(b.q_in.at[chips[dp], 64:192], b.k_in.at[chips[dp]], mate))
-    for one in sent_wo:
-        net.arrived(one)
-    sent_wo2 = {
-        (dp, dz): net.copy(
-            b.wo.at[planes[dz], chip, core], b.wo.at[planes[dz], chip, core], at(dp, 0)
-        )
-        for dz in (1, 2, 3)
-        for dp in (3, 1, 2)
-    }
-    make_mode(5)
-    make_mode(1)
-    l_cot.wait()
-
-    def mlp_grad(which):
-        b.mg[which] = (per_token(1, which) * b.cot[which].astype(F32)).astype(BF)
-
-    chunks(mlp_grad)
-    sent_mg = net.copy(b.mg, b.mg_in, mate)
-
-    for s in range(4):
-        b.qt[s, 0:64] = b.q_in[s, 0:64]
-        b.kt[s, 0:64] = b.q_in[s, 64:128]
-        b.vt[s] = b.q_in[s, 128:192]
-    for one in sent_k:
-        net.arrived(one)
-    for s in range(4):
-        b.kt[4 + s, 0:64] = b.k_in[s, 0:64]
-        b.vt[4 + s] = b.k_in[s, 64:128]
-    for s in range(8):
-        b.ka[s] = turned(b.kt[s]).astype(BF)
-
-    sent_h = {}
-    for dp in (3, 1, 2, 0):
-        q = chips[dp]
-        queries = b.qt[q]
-        peak = None
-        for s in range(8):
-            scores = dot(b.ka[s], queries)
-            b.scores[s] = scores
-            top = jnp.max(scores, axis=0, keepdims=True)
-            peak = top if peak is None else jnp.maximum(peak, top)
-        total = jnp.zeros((1, rows), F32)
-        result = jnp.zeros((64, rows), F32)
-        for s in range(8):
-            terms = jnp.exp2((b.scores[s] - peak) * EIGHTH_LOG2)
-            total = total + jnp.sum(terms, axis=0, keepdims=True)
-            low = terms.astype(BF)
-            b.terms[q, s] = low
-            result = result + dot(b.vt[s], low)
-        share = 1.0 / total
-        b.share[q] = share
-        result = result * share
-        b.heads[q] = result
-        b.h_out[q] = result.astype(BF)
-        for dz in (3, 2, 1, 0):
-            if dp or dz:
-                sent_h[dp, dz] = net.copy(
-                    b.h_out.at[q], b.h_in.at[plane, chip], at(dp, dz)
-                )
-    b.h_in[plane, chip] = b.h_out[chip]
-
-    for s in range(8):
-        b.vn[s] = turned(b.vt[s]).astype(BF)
-    for s in range(4):
-        b.qn[s] = turned(b.qt[s])[:, 0:64].astype(BF)
-    l_f2.wait()
-    for n in range(4):
-        cols = slice(n * 256, (n + 1) * 256)
-        b.dact[:, cols] = dot_nt(b.mg[...], b.f2[cols])
-    l_wo.wait()
-    for one in sent_wo2.values():
-        net.arrived(one)
-    sent_wo3 = [
-        net.copy(b.wo.at[planes[dz], :, core], b.wo.at[planes[dz], :, core], mate)
-        for dz in (1, 2, 3)
-    ]
-
-    for dz in range(4):
-        for dp in range(4):
-            if dp or dz:
-                net.arrived(sent_h[dp, dz])
-        if dz:
-            net.arrived(sent_wo3[dz - 1])
-        left = turned(b.h_in[planes[dz]].reshape(256, rows)).astype(BF)
-        right = b.wo[planes[dz]].reshape(256, width)
-        if dz:
-            b.attn[...] += dot(left, right)
-        else:
-            b.attn[...] = dot(left, right)
-    sent_hx = net.copy(b.h_in.at[plane, pl.ds(2 * other, 2)], b.h_mate, mate)
-
-
-    def second_norm(which):
-        value = b.tok[which].astype(F32) + per_token(0, which) * b.attn[which]
-        b.hid[which] = value
-        normed, _ = norm_rows(value)
-        value = (normed * (1.0 + per_token(3, which)) + per_token(5, which)).astype(BF)
-        b.b[0, which] = value[:, :half]
-        b.b[1, which] = value[:, half:]
-
-    chunks(second_norm)
-    l_f1.wait()
-    for n in range(4):
-        cols = slice(n * 256, (n + 1) * 256)
-        up = dot(b.b[0], b.f1[:half, cols]) + dot(b.b[1], b.f1[half:, cols])
-        square = up * up
-        bent = jnp.tanh(GELU_A * up * (1.0 + GELU_B * square))
-        gate = 0.5 * (1.0 + bent)
-        slope = gate + 0.5 * up * (1.0 - bent * bent) * (GELU_A * (1.0 + 3.0 * GELU_B * square))
-        b.act[n // 2, :, (n % 2) * 256 : (n % 2 + 1) * 256] = (up * gate).astype(BF)
-        b.ug[:, cols] = (b.dact[:, cols] * slope).astype(BF)
-    for n in range(4):
-        cols = slice(n * 256, (n + 1) * 256)
-        value = dot_nt(b.ug[...], b.f1[cols])
-        b.bg_out[:, :, cols] = value.astype(BF).reshape(4, own, 256)
-    sent_bg = [
-        net.copy(b.bg_out.at[planes[dz]], b.bg_in.at[dz - 1], at(0, dz)) for dz in (3, 2, 1)
-    ]
+    def summed(sent, kept, arrived):
+        for one in sent:
+            net.arrived(one)
+        total = kept.astype(F32)
+        for k in range(3):
+            total = total + arrived[k].astype(F32)
+        return total
 
     ways = ((0, 1, 2), (1, 2, 1))
 
@@ -395,6 +191,263 @@
             for way, first, then in ways
         ]
 
+    def plane_scatter(blocks, arrived, far):
+        far_sent = net.copy(blocks.at[planes[3]], far, at(0, 1), outer, inner)
+        sent = [
+            net.copy(blocks.at[planes[2]], arrived.at[1], at(0, 2), outer, inner),
+            net.copy(blocks.at[planes[3]], arrived.at[2], at(0, 3), inner, inner),
+            net.copy(blocks.at[planes[1]], arrived.at[0], at(0, 1)),
+        ]
+
+        @pl.when(outer)
+        def _():
+            arrived[2] = jnp.zeros(arrived.shape[1:], BF)
+
+        return sent, far_sent
+
+    def plane_scatter_on(far_sent, blocks, arrived, far):
+        net.arrived(far_sent)
+
+        @pl.when(inner)
+        def _():
+            total = blocks[planes[2]].astype(F32) + far[...].astype(F32)
+            blocks[planes[2]] = total.astype(BF)
+
+        return net.copy(blocks.at[planes[2]], arrived.at[1], at(0, 2), inner, outer)
+
+    def plane_gather(source, target):
+        return [
+            net.copy(source, target.at[plane], at(0, 2)),
+            net.copy(source, target.at[plane], at(0, 3), inner, inner),
+            net.copy(source, target.at[plane], at(0, 1)),
+        ]
+
+    def plane_gather_on(sent, target):
+        net.arrived(sent[0])
+        return net.copy(target.at[planes[2]], target.at[planes[2]], at(0, 1), inner, outer)
+
+    l_table = load(table_h, b.table)
+    l_ada = {k: load(ada_h.at[k], b.ada.at[k]) for k in (2, 4)}
+    l_tok = load(tok_h, b.tok)
+    l_wq = load(wq_h, b.wq)
+    barrier = pltpu.get_barrier_semaphore()
+    for dp, dz in offsets:
+        pl.semaphore_signal(barrier, inc=1, device_id=at(dp, dz), device_id_type=MESH)
+    pl.semaphore_signal(barrier, inc=1, device_id=mate, device_id_type=MESH)
+
+    spot = lax.rem(lax.broadcasted_iota(jnp.int32, (3 * ITEM_ROWS, rows), 0), ITEM_ROWS)
+    picks = jnp.where(spot == item_v[group], 1.0, 0.0)
+    b.pick[...] = picks.T.astype(BF)
+
+    spot = lax.broadcasted_iota(jnp.int32, (ITEM_ROWS, classes), 0)
+    label = lax.broadcasted_iota(jnp.int32, (ITEM_ROWS, classes), 1)
+    hot = jnp.zeros((ITEM_ROWS, classes), F32)
+    for i in range(items):
+        hot = jnp.where((spot == i) & (label == cls_s[i]), 1.0, hot)
+    l_table.wait()
+    cond = dot(hot.astype(BF), b.table[...])
+    b.cond[...] = cond
+    cond_low = (cond / (1.0 + jnp.exp(-cond))).astype(BF)
+
+    def make_mode(k):
+        l_ada[k].wait()
+        value = dot(cond_low, b.ada[k])
+        high = value.astype(BF)
+        rest = value - high.astype(F32)
+        middle = rest.astype(BF)
+        b.modes[k, 0:ITEM_ROWS] = high
+        b.modes[k, ITEM_ROWS : 2 * ITEM_ROWS] = middle
+        b.modes[k, 2 * ITEM_ROWS : 3 * ITEM_ROWS] = (rest - middle.astype(F32)).astype(BF)
+
+    def per_token(k, which):
+        return dot(b.pick[which], b.modes[k])
+
+    def chunks(body):
+        def step(i, carry):
+            body(pl.ds(pl.multiple_of(i * 64, 64), 64))
+            return carry
+
+        lax.fori_loop(0, rows // 64, step, 0)
+
+    make_mode(2)
+    make_mode(4)
+
+    l_tok.wait()
+
+    def first_norm(which):
+        normed, _ = norm_rows(b.tok[which].astype(F32))
+        value = (normed * (1.0 + per_token(2, which)) + per_token(4, which)).astype(BF)
+        b.a[0, which] = value[:, :half]
+        b.a[1, which] = value[:, half:]
+
+    for i in range(0, rows, 64):
+        first_norm(slice(i, i + 64))
+    l_wq.wait()
+    l_wo = load(wo_h, b.wo.at[plane])
+    l_ada.update({k: load(ada_h.at[k], b.ada.at[k]) for k in (0, 3, 5, 1)})
+    l_cot = load(cot_h, b.cot)
+    l_f2 = load(f2_h, b.f2)
+    l_f1 = load(f1_h, b.f1)
+    first_store = len(loads)
+    for k in range(3):
+        value = dot(b.a[0], b.wq[k, :half]) + dot(b.a[1], b.wq[k, half:])
+        value = value.T.astype(BF)
+        for h in range(4):
+            b.q_out[h, k * 64 : (k + 1) * 64] = value[h * 64 : (h + 1) * 64]
+    pl.semaphore_wait(barrier, len(offsets) + 1)
+    sent_q = {
+        (dp, n): net.copy(b.q_out.at[chips[dp], part_of], b.q_in.at[dp, part_of], at(dp, 0))
+        for n, part_of in enumerate((slice(64, 192), slice(0, 64)))
+        for dp in (3, 1, 2)
+    }
+    b.q_in[0] = b.q_out[chip]
+    sent_k = [net.copy(b.q_in.at[0, 64:192], b.k_in.at[0], mate)]
+    sent_a = net.copy(b.a.at[other], b.a_in, mate)
+    sent_wo = [
+        net.copy(wo_h.at[chip, core], b.wo.at[plane, chip, core], at(0, dz)) for dz in (3, 2, 1)
+    ]
+
+    spot = lax.broadcasted_iota(jnp.int32, (64, rows), 0)
+    for s in range(4):
+        for k, parity in enumerate((core, other)):
+            item, scale = item_v[chips[s] * 2 + parity], scale_v[chips[s] * 2 + parity]
+            by_item = jnp.where(item != spot - 1, BARRED, 0.0)
+            by_scale = jnp.where((spot < 32) & (scale > spot - 16), BARRED, 0.0)
+            b.kt[k * 4 + s, 64:128] = jnp.where(spot < 16, by_item, by_scale).astype(BF)
+        item, scale = item_v[chips[s] * 2 + core], scale_v[chips[s] * 2 + core]
+        by_item = jnp.where(item == spot - 1, 1.0, 0.0)
+        by_scale = jnp.where((spot < 32) & (scale == spot - 16), 1.0, 0.0)
+        b.qt[s, 64:128] = jnp.where(spot < 16, by_item, by_scale).astype(BF)
+    make_mode(0)
+    make_mode(3)
+    make_mode(5)
+    make_mode(1)
+    l_cot.wait()
+
+    def mlp_grad(which):
+        b.mg[which] = (per_token(1, which) * b.cot[which].astype(F32)).astype(BF)
+
+    chunks(mlp_grad)
+    for dp in (3, 1, 2):
+        net.arrived(sent_q[dp, 0])
+        sent_k.append(net.copy(b.q_in.at[dp, 64:192], b.k_in.at[dp], mate))
+
+    def take_keys(s, block):
+        b.kt[s, 0:64] = block[0:64]
+        b.ktw[:, s * 256 : (s + 1) * 256] = block[0:64]
+        b.vt[s] = block[64:128]
+        b.ka[s] = turned(b.kt[s]).astype(BF)
+
+    for s in range(4):
+        take_keys(s, b.q_in[s, 64:192])
+    for dp in (3, 1, 2):
+        net.arrived(sent_q[dp, 1])
+    for s in range(4):
+        b.qt[s, 0:64] = b.q_in[s, 0:64]
+    for one in sent_k:
+        net.arrived(one)
+    for s in range(4):
+        take_keys(4 + s, b.k_in[s])
+    sent_mg = net.copy(b.mg, b.mg_in, mate)
+
+    sent_h = {}
+    for dp in (3, 1, 2, 0):
+        queries = b.qt[dp]
+        peak = None
+        for s in range(8):
+            scores = dot(b.ka[s], queries)
+            b.scores[s] = scores
+            top = jnp.max(scores, axis=0, keepdims=True)
+            peak = top if peak is None else jnp.maximum(peak, top)
+        total = jnp.zeros((1, rows), F32)
+        result = jnp.zeros((64, rows), F32)
+        cols = slice(dp * 256, (dp + 1) * 256)
+        for s in range(8):
+            terms = jnp.exp2((b.scores[s] - peak) * EIGHTH_LOG2)
+            total = total + jnp.sum(terms, axis=0, keepdims=True)
+            low = terms.astype(BF)
+            b.pairs[s * 256 : (s + 1) * 256, 1024 + dp * 256 : 1280 + dp * 256] = low
+            result = result + dot(b.vt[s], low)
+        share = 1.0 / total
+        b.share[:, cols] = share
+        result = result * share
+        b.heads[:, cols] = result
+        b.h_out[dp] = result.astype(BF)
+        for dz in (3, 2, 1, 0):
+            if dp or dz:
+                sent_h[dp, dz] = net.copy(b.h_out.at[dp], b.h_in.at[plane, chip], at(dp, dz))
+        if dp == 3:
+            for one in sent_wo:
+                net.arrived(one)
+            sent_wo2 = {
+                (to, dz): net.copy(
+                    b.wo.at[planes[dz], chip, core], b.wo.at[planes[dz], chip, core], at(to, 0)
+                )
+                for dz in (1, 2, 3)
+                for to in (3, 1, 2)
+            }
+    b.h_in[plane, chip] = b.h_out[0]
+
+    for s in range(8):
+        b.vn[s] = turned(b.vt[s]).astype(BF)
+    for s in range(4):
+        some = turned(b.q_in[s, 0:64])
+        b.wide[s * 256 : (s + 1) * 256] = jnp.concatenate(
+            [some * 0.125, jnp.zeros((rows, 64), F32)], axis=1
+        ).astype(BF)
+    l_f2.wait()
+    for n in range(4):
+        cols = slice(n * 256, (n + 1) * 256)
+        b.dact[:, cols] = dot_nt(b.mg[...], b.f2[cols])
+    l_wo.wait()
+    for one in sent_wo2.values():
+        net.arrived(one)
+    sent_wo3 = [
+        net.copy(b.wo.at[planes[dz], :, core], b.wo.at[planes[dz], :, core], mate)
+        for dz in (1, 2, 3)
+    ]
+
+    for dz in range(4):
+        for dp in range(4):
+            if dp or dz:
+                net.arrived(sent_h[dp, dz])
+        if dz:
+            net.arrived(sent_wo3[dz - 1])
+        left = turned(b.h_in[planes[dz]].reshape(256, rows)).astype(BF)
+        right = b.wo[planes[dz]].reshape(256, width)
+        if dz:
+            b.attn[...] += dot(left, right)
+        else:
+            b.attn[...] = dot(left, right)
+    sent_hx = net.copy(b.h_in.at[plane, pl.ds(2 * other, 2)], b.h_mate, mate)
+
+
+    def second_norm(which):
+        value = b.tok[which].astype(F32) + per_token(0, which) * b.attn[which]
+        b.hid[which] = value
+        normed, _ = norm_rows(value)
+        value = (normed * (1.0 + per_token(3, which)) + per_token(5, which)).astype(BF)
+        b.b[0, which] = value[:, :half]
+        b.b[1, which] = value[:, half:]
+
+    for i in range(0, rows, 64):
+        second_norm(slice(i, i + 64))
+    l_f1.wait()
+    for n in range(4):
+        cols = slice(n * 256, (n + 1) * 256)
+        up = dot(b.b[0], b.f1[:half, cols]) + dot(b.b[1], b.f1[half:, cols])
+        square = up * up
+        bent = jnp.tanh(GELU_A * up * (1.0 + GELU_B * square))
+        gate = 0.5 * (1.0 + bent)
+        slope = gate + 0.5 * up * (1.0 - bent * bent) * (GELU_A * (1.0 + 3.0 * GELU_B * square))
+        b.act[n // 2, :, (n % 2) * 256 : (n % 2 + 1) * 256] = (up * gate).astype(BF)
+        b.ug[:, cols] = (b.dact[:, cols] * slope).astype(BF)
+    for n in range(4):
+        cols = slice(n * 256, (n + 1) * 256)
+        value = dot_nt(b.ug[...], b.f1[cols])
+        b.bg_out[:, :, cols] = value.astype(BF).reshape(4, own, 256)
+    sent_bg, far_bg = plane_scatter(b.bg_out, b.bg_in, b.bg_far)
+
     sent_x = [
         net.copy(b.act.at[other], b.act_in, mate),
         net.copy(b.b.at[other], b.b_in, mate),
@@ -409,6 +462,7 @@
         value = dot(b.left[0, some], b.mg[...]) + dot(b.left[1, some], b.mg_in[...])
         b.g2_out[n] = value.astype(BF).reshape(2, 64, width)
     sent_g2 = scatter(b.g2_out, b.g2_in)
+    sent_bg.append(plane_scatter_on(far_bg, b.bg_out, b.bg_in, b.bg_far))
     b.left[0] = turned(b.b[core]).astype(BF)
     net.arrived(sent_x[1])
     b.left[1] = turned(b.b_in[...]).astype(BF)
@@ -423,14 +477,6 @@
         value = dot(b.act[0], b.f2[:half, cols]) + dot(b.act[1], b.f2[half:, cols])
         b.mo_out[:, :, cols] = value.astype(BF).reshape(4, own, 256)
 
-    def summed(sent, kept, arrived):
-        for one in sent:
-            net.arrived(one)
-        total = kept.astype(F32)
-        for k in range(3):
-            total = total + arrived[k].astype(F32)
-        return total
-
     def mode_sums(k, value):
         high = value.astype(BF)
         low = (value - high.astype(F32)).astype(BF)
@@ -438,41 +484,6 @@
         value = (dot(picked, high) + dot(picked, low))[0:8]
         b.ms[0, k * 8 : (k + 1) * 8] = value[:, :half]
         b.ms[1, k * 8 : (k + 1) * 8] = value[:, half:]
-
-    def plane_scatter(blocks, arrived, far):
-        far_sent = net.copy(blocks.at[planes[3]], far, at(0, 1), outer, inner)
-        sent = [
-            net.copy(blocks.at[planes[2]], arrived.at[1], at(0, 2), outer, inner),
-            net.copy(blocks.at[planes[3]], arrived.at[2], at(0, 3), inner, inner),
-            net.copy(blocks.at[planes[1]], arrived.at[0], at(0, 1)),
-        ]
-
-        @pl.when(outer)
-        def _():
-            arrived[2] = jnp.zeros(arrived.shape[1:], BF)
-
-        return sent, far_sent
-
-    def plane_scatter_on(far_sent, blocks, arrived, far):
-        net.arrived(far_sent)
-
-        @pl.when(inner)
-        def _():
-            total = blocks[planes[2]].astype(F32) + far[...].astype(F32)
-            blocks[planes[2]] = total.astype(BF)
-
-        return net.copy(blocks.at[planes[2]], arrived.at[1], at(0, 2), inner, outer)
-
-    def plane_gather(source, target):
-        return [
-            net.copy(source, target.at[plane], at(0, 2)),
-            net.copy(source, target.at[plane], at(0, 3), inner, inner),
-            net.copy(source, target.at[plane], at(0, 1)),
-        ]
-
-    def plane_gather_on(sent, target):
-        net.arrived(sent[0])
-        return net.copy(target.at[planes[2]], target.at[planes[2]], at(0, 1), inner, outer)
 
     b_grad = summed(sent_bg, b.bg_out[plane], b.bg_in)
     normed, inverse = norm_rows(b.hid[mine])
@@ -489,11 +500,13 @@
             b.do_out[n, h] = jnp.concatenate([some[: own // 2], some[own // 2 :]], axis=1)
     sent_do = {
         (dp, dz): net.copy(
-            b.do_out.at[planes[dz], chips[dp]], b.do_in.at[chip, plane], at(dp, dz)
+            b.do_out.at[planes[dz], chips[dp]], b.do_in.at[dp, plane], at(dp, dz)
         )
         for dp, dz in reversed(offsets)
     }
-    b.do_in[chip, plane] = b.do_out[plane, chip]
+    b.do_in[0, plane] = b.do_out[plane, chip]
+    sent_mo, far_mo = plane_scatter(b.mo_out, b.mo_in, b.mo_far)
+    sent_ag = plane_gather(b.ag.at[plane], b.ag)
     mode_sums(0, h_grad * b.attn[mine])
     mode_sums(3, b_grad * normed)
     mode_sums(5, b_grad)
@@ -502,47 +515,50 @@
 
     for one in sent_do.values():
         net.arrived(one)
-    sent_mo, far_mo = plane_scatter(b.mo_out, b.mo_in, b.mo_far)
-    sent_ag = plane_gather(b.ag.at[plane], b.ag)
     for s in range(4):
+        cols = slice(s * 256, (s + 1) * 256)
         for n in range(4):
             both = b.do_in[s, n]
-            b.dn[s, n * own : n * own + own // 2] = both[:, 0:64]
-            b.dn[s, n * own + own // 2 : (n + 1) * own] = both[:, 64:128]
-        value = turned(b.dn[s])
-        b.dt[s] = value.astype(BF)
-        b.delta[s] = jnp.sum(value * b.heads[s], axis=0, keepdims=True)
-        b.dn[s] = (value * b.share[s]).T.astype(BF)
-        b.dq[s] = jnp.zeros((64, rows), F32)
-
-    def attend_back(s, carry):
-        keys, values = b.kt[s, 0:64], b.vn[s]
-        key_grad = jnp.zeros((rows, 64), F32)
-        value_grad = jnp.zeros((rows, 64), F32)
+            b.dn[n * own : n * own + own // 2] = both[:, 0:64]
+            b.dn[n * own + own // 2 : (n + 1) * own] = both[:, 64:128]
+        value = turned(b.dn[...])
+        b.dt[:, cols] = value.astype(BF)
+        b.delta[:, cols] = jnp.sum(value * b.heads[:, cols], axis=0, keepdims=True)
+        b.wide[1024 + s * 256 : 1280 + s * 256] = jnp.concatenate(
+            [jnp.zeros((rows, 64), F32), (value * b.share[:, cols]).T], axis=1
+        ).astype(BF)
+
+    def attend_back(s):
+        keys = slice(s * 256, (s + 1) * 256)
         for q in range(4):
-            terms = b.terms[q, s]
-            pull = (dot(values, b.dt[q]) - b.delta[q]) * b.share[q]
-            low = (pull * terms.astype(F32)).astype(BF)
-            b.dq[q] += dot(keys, low)
-            key_grad = key_grad + dot(low, b.qn[q])
-            value_grad = value_grad + dot(terms, b.dn[q])
-        b.dkv[s] = jnp.concatenate([key_grad * 0.125, value_grad], axis=1).T
-        return carry
-
-    lax.fori_loop(4, 8, attend_back, 0)
+            cols = slice(q * 256, (q + 1) * 256)
+            pull = (dot(b.vn[s], b.dt[:, cols]) - b.delta[:, cols]) * b.share[:, cols]
+            terms = b.pairs[keys, 1024 + q * 256 : 1280 + q * 256]
+            b.pairs[keys, cols] = (pull * terms.astype(F32)).astype(BF)
+        b.dkv[s] = dot(b.pairs[keys], b.wide[...]).T
+
+    for s in range(4, 8):
+        attend_back(s)
     sent_dkv = net.copy(b.dkv.at[4:8], b.dkv_in, mate)
+    for s in range(4):
+        attend_back(s)
+    value = (dot(b.ktw[...], b.pairs[:, 0:1024]) * 0.125).astype(BF)
+    for s in range(4):
+        b.dx_out[s, 0:64] = value[:, s * 256 : (s + 1) * 256]
+    b.dx_in[chip, 0:64] = b.dx_out[0, 0:64]
+    sent_dx = [
+        net.copy(b.dx_out.at[dp, 0:64], b.dx_in.at[chip, 0:64], at(dp, 0)) for dp in (3, 1, 2)
+    ]
+    net.arrived(sent_dkv)
+    for s in range(4):
+        b.dx_out[s, 64:192] = (b.dkv[s] + b.dkv_in[s]).astype(BF)
+    b.dx_in[chip, 64:192] = b.dx_out[0, 64:192]
+    sent_dx += [
+        net.copy(b.dx_out.at[dp, 64:192], b.dx_in.at[chip, 64:192], at(dp, 0)) for dp in (3, 1, 2)
+    ]
     sent_mo.append(plane_scatter_on(far_mo, b.mo_out, b.mo_in, b.mo_far))
     sent_g2b = gather(sent_g2, b.g2_out, b.g2_in, b.g2, gf2_o)
     sent_g1b = gather(sent_g1, b.g1_out, b.g1_in, b.g1, gf1_o)
-    lax.fori_loop(0, 4, attend_back, 0)
-    net.arrived(sent_dkv)
-    for s in range(4):
-        b.dx_out[s, 0:64] = (b.dq[s] * 0.125).astype(BF)
-        b.dx_out[s, 64:192] = (b.dkv[s] + b.dkv_in[s]).astype(BF)
-    sent_dx = [
-        net.copy(b.dx_out.at[chips[dp]], b.dx_in.at[chip], at(dp, 0)) for dp in (3, 1, 2)
-    ]
-    b.dx_in[chip] = b.dx_out[chip]
     sent_ag.append(plane_gather_on(sent_ag, b.ag))
 
     for one in sent_dx:
@@ -557,9 +573,7 @@
         value = value + dot_nt(b.dx[1], b.wq[1, cols])
         value = value + dot_nt(b.dx[2], b.wq[2, cols])
         b.xg_out[:, :, cols] = value.astype(BF).reshape(4, own, 256)
-    sent_xg = [
-        net.copy(b.xg_out.at[planes[dz]], b.xg_in.at[dz - 1], at(0, dz)) for dz in (3, 2, 1)
-    ]
+    sent_xg, far_xg = plane_scatter(b.xg_out, b.xg_in, b.xg_far)
 
     net.arrived(sent_a)
     net.arrived(sent_dxm)
@@ -567,6 +581,7 @@
         value = dot(b.dx_in[h], b.a[core]) + dot(b.dx_mate[h], b.a_in[...])
         b.gq_out[h] = value.astype(BF).reshape(2, 96, half)
     sent_gq = scatter(b.gq_out, b.gq_in)
+    sent_xg.append(plane_scatter_on(far_xg, b.xg_out, b.xg_in, b.xg_far))
 
     sent_g2b += gather_on(sent_g2b, gf2_o)
     sent_g1b += gather_on(sent_g1b, gf1_o)
@@ -591,8 +606,8 @@
         net.copy(b.go_out.at[chips[dp]], b.go_in.at[dp - 1], at(dp, 0)) for dp in (3, 1, 2)
     ]
 
+    sent_gq = scatter_on(sent_gq, b.gq_out, b.gq_in)
     plane_gather_on(sent_out, out_o)
-    sent_gq = scatter_on(sent_gq, b.gq_out, b.gq_in)
 
     a_grad = summed(sent_xg, b.xg_out[plane], b.xg_in)
     normed, inverse = norm_rows(b.tok[mine].astype(F32))
@@ -614,23 +629,36 @@
     net.copy(b.go, gout_o.at[core, chip], mate)
     b.m2[...] = summed(sent_m1, b.m1[...], b.m1_in).astype(BF)
     sent_m2 = [net.copy(b.m2, b.m2_in.at[dp - 1], at(dp, 0)) for dp in (3, 1, 2)]
-    b.m3[...] = summed(sent_m2, b.m2[...], b.m2_in)
-    net.copy(b.m3, mode_o.at[core], mate)
-    load(b.m3, mode_o.at[core])
-    load(b.cond, cond_o)
-    sent_gqb += gather_on(sent_gqb, gqkv_o)
     plane_gather_on(sent_dt, dtok_o)
 
-    for sent, array in ((sent_g2b, gf2_o), (sent_g1b, gf1_o), (sent_gqb, gqkv_o)):
-        for one in sent[2:]:
+    def pass_on(sent, array):
+        for one in sent:
             net.arrived(one)
         for dp in (1, 2, 3):
             where = (core, chips[dp])
             net.copy(array.at[where], array.at[where], mate)
-    for one, dp in zip(sent_gob, (3, 1, 2), strict=True):
-        net.arrived(one)
-        where = (core, chips[dp])
-        net.copy(gout_o.at[where], gout_o.at[where], mate)
+
+    pass_on(sent_g2b[2:], gf2_o)
+    pass_on(sent_g1b[2:], gf1_o)
+    sent_gqb += gather_on(sent_gqb, gqkv_o)
+    b.m3[...] = summed(sent_m2, b.m2[...], b.m2_in)
+    net.copy(b.m3, mode_o.at[core], mate)
+    load(b.m3, mode_o.at[core])
+    some = pl.ds(pl.multiple_of(plane * part, part), part)
+    side = pl.ds(pl.multiple_of(core * half, half), half)
+    value = jnp.zeros((16, part), F32)
+    for k in range(COMPONENTS):
+        sums = b.m3[k * 8 : (k + 1) * 8]
+        high = sums.astype(BF).astype(F32)
+        both = jnp.concatenate([high, sums - high], axis=0).astype(BF)
+        value = value + dot_nt(both, b.ada[k, some, side])
+    b.cg[...] = value[0:8] + value[8:16]
+    net.copy(b.cg, cg_o.at[core], mate)
+    load(b.cg, cg_o.at[core])
+    load(b.cond, cond_o)
+    pass_on(sent_gob, gout_o)
+    pass_on(sent_gqb[2:], gqkv_o)
+    assert len(net.made) == COPIES and len(loads) == LOADS
     net.finish()
     for one in loads[first_store:]:
         one.wait()
@@ -661,11 +689,12 @@
         vt=((8, 64, rows), BF),
         vn=((8, rows, 64), BF),
         qt=((4, 128, rows), BF),
-        qn=((4, rows, 64), BF),
+        ktw=((64, 2048), BF),
+        wide=((2048, 128), BF),
         scores=((8, rows, rows), F32),
-        terms=((4, 8, rows, rows), BF),
-        share=((4, 1, rows), F32),
-        heads=((4, 64, rows), F32),
+        pairs=((2048, 2048), BF),
+        share=((1, 1024), F32),
+        heads=((64, 1024), F32),
         h_out=((4, 64, rows), BF),
         h_in=((4, 4, 64, rows), BF),
         h_mate=((2, 64, rows), BF),
@@ -686,6 +715,8 @@
         mo_out=((4, own, width), BF),
         mo_in=((3, own, width), BF),
         mo_far=((own, width), BF),
+        bg_far=((own, width), BF),
+        xg_far=((own, width), BF),
         xg_out=((4, own, width), BF),
         xg_in=((3, own, width), BF),
         g1_out=((4, 2, 64, width), BF),
@@ -699,10 +730,9 @@
         ag_in=((4, own, width), BF),
         do_out=((4, 4, own // 2, 128), BF),
         do_in=((4, 4, own // 2, 128), BF),
-        dn=((4, rows, 64), BF),
-        dt=((4, 64, rows), BF),
-        delta=((4, 1, rows), F32),
-        dq=((4, 64, rows), F32),
+        dn=((rows, 64), BF),
+        dt=((64, 1024), BF),
+        delta=((1, 1024), F32),
         dkv=((8, 128, rows), F32),
         dkv_in=((4, 128, rows), F32),
         dx_out=((4, 192, rows), BF),
@@ -724,26 +754,18 @@
         m2=((48, half), BF),
         m2_in=((3, 48, half), BF),
         m3=((48, half), F32),
+        cg=((8, part), F32),
     )
 
 
 def finish_kernel(
-    cls_s, ada_h, out_i, dtok_i, gqkv_i, gout_i, gf1_i, gf2_i, mode_i, cond_i,
-    out_o, dtok_o, table_o, ada_o, qkv_o, wout_o, f1_o, f2_o, ada_v, sems,
+    cls_s, out_i, dtok_i, gqkv_i, gout_i, gf1_i, gf2_i, mode_i, cond_i, cg_i,
+    out_o, dtok_o, table_o, ada_o, qkv_o, wout_o, f1_o, f2_o,
 ):
     step, last = pl.program_id(0), pl.num_programs(0) - 1
     plane = lax.axis_index("head")
     part = table_o.shape[1]
     mine = pl.ds(pl.multiple_of(plane * part, part), part)
-    fetch = [
-        pltpu.make_async_copy(ada_h.at[k, mine], ada_v.at[k], sems.at[k]) for k in range(COMPONENTS)
-    ]
-
-    @pl.when(step == 0)
-    def _():
-        for one in fetch:
-            one.start()
-
     out_o[...] = out_i[0]
     dtok_o[...] = dtok_i[0]
     wout_o[...] = gout_i[0, 0].astype(F32)
@@ -764,18 +786,9 @@
 
     @pl.when(step == last)
     def _():
-        cond_grad = jnp.zeros((16, part), F32)
-        half = mode_i.shape[2]
-        for k in range(COMPONENTS):
-            fetch[k].wait()
-            for n in range(2):
-                value = mode_i[n, k * 8 : (k + 1) * 8]
-                high = value.astype(BF).astype(F32)
-                both = jnp.concatenate([high, value - high], axis=0).astype(BF)
-                cond_grad = cond_grad + dot_nt(both, ada_v[k, :, n * half : (n + 1) * half])
         own = cond_i[0:8, mine]
         gate = 1.0 / (1.0 + jnp.exp(-own))
-        grad = (cond_grad[0:8] + cond_grad[8:16]) * gate * (1.0 + own * (1.0 - gate))
+        grad = (cg_i[0] + cg_i[1]) * gate * (1.0 + own * (1.0 - gate))
         spot = lax.broadcasted_iota(jnp.int32, table_o.shape, 0)
         total = jnp.zeros(table_o.shape, F32)
         for i in range(cls_s.shape[0]):
@@ -784,13 +797,22 @@
 
 
 def finish(
-    class_ids, w_ada, output, d_tokens, qkv_sum, out_sum, fc1_sum, fc2_sum, mode_grad, cond, classes
+    class_ids,
+    output,
+    d_tokens,
+    qkv_sum,
+    out_sum,
+    fc1_sum,
+    fc2_sum,
+    mode_grad,
+    cond,
+    cond_grad,
+    classes,
 ):
     steps = 8
     own, width = output.shape[1:]
     half, part, hidden = width // 2, width // 4, steps * 128
     rows = own * 4
-    anywhere = pl.BlockSpec(memory_space=pl.ANY)
     smem = pl.BlockSpec(memory_space=pltpu.SMEM)
     few = pl.BlockSpec((1, own // 2, width), lambda i: (i // 2, i % 2, 0))
     table, ada, qkv, out, fc1, fc2 = (
@@ -811,7 +833,6 @@
         + [jax.ShapeDtypeStruct(shape, F32) for shape in (table, ada, qkv, out, fc1, fc2)],
         in_specs=[
             smem,
-            anywhere,
             few,
             few,
             pl.BlockSpec((1, 4, 2, 96, half // 4), lambda i: (i // 4, 0, 0, 0, i % 4)),
@@ -820,6 +841,7 @@
             pl.BlockSpec((1, 1, 2, 64, width), lambda i: (i // 4, i % 4, 0, 0, 0)),
             pl.BlockSpec((2, 48, half), lambda i: (0, 0, 0)),
             pl.BlockSpec((ITEM_ROWS, width), lambda i: (0, 0)),
+            pl.BlockSpec((2, 8, part), lambda i: (0, 0, 0)),
         ],
         out_specs=[
             pl.BlockSpec((rows // steps, width), lambda i: (i, 0)),
@@ -831,13 +853,9 @@
             pl.BlockSpec((128, hidden), lambda i: (i, 0)),
             pl.BlockSpec((128, width), lambda i: (i, 0)),
         ],
-        scratch_shapes=[
-            pltpu.VMEM((COMPONENTS, part, width), BF),
-            pltpu.SemaphoreType.DMA((COMPONENTS,)),
-        ],
         compiler_params=pltpu.CompilerParams(vmem_limit_bytes=VMEM_BYTES),
     )(
-        class_ids, w_ada, output, d_tokens, qkv_sum, out_sum, fc1_sum, fc2_sum, mode_grad, cond
+        class_ids, output, d_tokens, qkv_sum, out_sum, fc1_sum, fc2_sum, mode_grad, cond, cond_grad
     )
     return output, d_tokens, table, ada, qkv.transpose(1, 0, 2), out, fc1, fc2
 
@@ -864,7 +882,7 @@
     anywhere = pl.BlockSpec(memory_space=pl.ANY)
     vmem = pl.BlockSpec(memory_space=pltpu.VMEM)
     smem = pl.BlockSpec(memory_space=pltpu.SMEM)
-    output, d_tokens, qkv_sum, out_sum, fc1_sum, fc2_sum, mode_grad, cond = pl.pallas_call(
+    output, d_tokens, qkv_sum, out_sum, fc1_sum, fc2_sum, mode_grad, cond, cond_grad = pl.pallas_call(
         functools.partial(block_kernel, dims),
         out_shape=[
             jax.ShapeDtypeStruct((4, own, width), BF),
@@ -875,13 +893,14 @@
             jax.ShapeDtypeStruct((2, 4, 2, 64, width), BF),
             jax.ShapeDtypeStruct((2, 48, half), F32),
             jax.ShapeDtypeStruct((ITEM_ROWS, width), F32),
+            jax.ShapeDtypeStruct((2, 8, part), F32),
         ],
         in_specs=[anywhere, smem, vmem, vmem] + [anywhere] * 7,
-        out_specs=[anywhere] * 8,
+        out_specs=[anywhere] * 9,
         scratch_shapes=[
             pltpu.SemaphoreType.DMA((COPIES,)),
             pltpu.SemaphoreType.DMA((COPIES,)),
-            pltpu.SemaphoreType.DMA((32,)),
+            pltpu.SemaphoreType.DMA((LOADS,)),
             *scratch,
         ],
         compiler_params=pltpu.CompilerParams(
@@ -904,7 +923,7 @@
         cotangent,
     )
     return finish(
-        class_ids, w_ada, output, d_tokens, qkv_sum, out_sum, fc1_sum, fc2_sum, mode_grad, cond,
+        class_ids, output, d_tokens, qkv_sum, out_sum, fc1_sum, fc2_sum, mode_grad, cond, cond_grad,
         classes,
     )
 

time: 137 us -> 124 us (0.905)
  Pallas kernels: 136 us -> 123 us
    pallas_call x1, Pallas kernels: 120 us -> 111 us  [on_block(): pl.pallas_call(functools.partial(block_kernel, dims), out_shape=[jax.Shap...]
    pallas_call x1, Pallas kernels: 16.3 us -> 12.4 us  [finish(): pl.pallas_call(finish_kernel, grid=(steps,), out_shape=[jax.ShapeDtypeStr...]
where the time goes in v3:
time: 124 us
  Pallas kernels  123 us (99%)
    pallas_call x1, Pallas kernels, on_block(): pl.pallas_call(functools.partial(block_kernel, dims), out_shape=[jax.Shap...  111 us
    pallas_call x1, Pallas kernels, finish(): pl.pallas_call(finish_kernel, grid=(steps,), out_shape=[jax.ShapeDtypeStr...  12.4 us

profile of v3, /device:TPU:0, one launch (start us, length us, event | category | flops | bytes accessed | tf_op | source)
XLA Modules:
  0.0 124.0 jit_solution(14005586576750344591)
XLA Ops:
  0.6 110.8 %shard_map.170 = (bf16[4,64,1024]{2,1,0:T(8,128)(2,1)}, bf16[4,64,1024]{2,1,0:T(8,128)(2,1)}, bf16[2,4,2,96,512]{4,3,2,1,0:T(8,128)(2,1)}, bf16[2,4,32,1024]{3,2...) custom-call(bf16[256,1024]{1,0:T(8,128)(2,1)} %refs_0_.1, ...), custom_call_target="tpu_custom_call" | custom-call | flops 10000000000 | bytes 40000000 | tf_op jit(solution)/shard_map/pallas_call | solution.py:885
  111.5 12.4 %shard_map.171 = (bf16[256,1024]{1,0:T(8,128)(2,1)}, bf16[256,1024]{1,0:T(8,128)(2,1)}, f32[1000,256]{1,0:T(8,128)}, f32[6,1024,256]{2,1,0:T(8,128)}, f32[3,1024...) custom-call(s32[3]{0:T(128)} %cls_s.1, ...), custom_call_target="tpu_custom_call" | custom-call | tf_op jit(solution)/shard_map/pallas_call | solution.py:826

commit v4 on v3

--- a/solution.py
+++ b/solution.py
@@ -768,13 +768,13 @@
     mine = pl.ds(pl.multiple_of(plane * part, part), part)
     out_o[...] = out_i[0]
     dtok_o[...] = dtok_i[0]
-    wout_o[...] = gout_i[0, 0].astype(F32)
-    f1_o[...] = gf1_i[0, 0].astype(F32).reshape(f1_o.shape)
-    f2_o[...] = gf2_i[0, 0].astype(F32).reshape(f2_o.shape)
-    sums = gqkv_i[0].astype(F32).reshape(4, 192, 128)
+    wout_o[...] = gout_i[0].astype(F32).reshape(wout_o.shape)
+    f1_o[...] = gf1_i[0].astype(F32).reshape(f1_o.shape)
+    f2_o[...] = gf2_i[0].astype(F32).reshape(f2_o.shape)
+    sums = gqkv_i[0].astype(F32).reshape(4, 192, 256)
     for k in range(3):
-        qkv_o[k] = sums[:, k * 64 : (k + 1) * 64].reshape(part, 128).T
-    cond = cond_i[:, pl.ds(pl.multiple_of(step * 128, 128), 128)]
+        qkv_o[k] = sums[:, k * 64 : (k + 1) * 64].reshape(part, 256).T
+    cond = cond_i[:, pl.ds(pl.multiple_of(step * 256, 256), 256)]
     cond_low = (cond / (1.0 + jnp.exp(-cond)))[0:8]
     low = jnp.concatenate([cond_low, cond_low], axis=0).astype(BF)
     side = pl.ds(pl.multiple_of(lax.rem(plane, 2) * part, part), part)
@@ -809,12 +809,12 @@
     cond_grad,
     classes,
 ):
-    steps = 8
+    steps = 4
     own, width = output.shape[1:]
-    half, part, hidden = width // 2, width // 4, steps * 128
+    half, part, hidden = width // 2, width // 4, 1024
     rows = own * 4
     smem = pl.BlockSpec(memory_space=pltpu.SMEM)
-    few = pl.BlockSpec((1, own // 2, width), lambda i: (i // 2, i % 2, 0))
+    few = pl.BlockSpec((1, own, width), lambda i: (i, 0, 0))
     table, ada, qkv, out, fc1, fc2 = (
         (classes, part),
         (COMPONENTS, width, part),
@@ -835,10 +835,10 @@
             smem,
             few,
             few,
-            pl.BlockSpec((1, 4, 2, 96, half // 4), lambda i: (i // 4, 0, 0, 0, i % 4)),
-            pl.BlockSpec((1, 1, 32, width), lambda i: (i // 4, i % 4, 0, 0)),
-            pl.BlockSpec((1, 1, 2, 64, hidden), lambda i: (i // 4, i % 4, 0, 0, 0)),
-            pl.BlockSpec((1, 1, 2, 64, width), lambda i: (i // 4, i % 4, 0, 0, 0)),
+            pl.BlockSpec((1, 4, 2, 96, half // 2), lambda i: (i // 2, 0, 0, 0, i % 2)),
+            pl.BlockSpec((1, 2, 32, width), lambda i: (i // 2, i % 2, 0, 0)),
+            pl.BlockSpec((1, 2, 2, 64, hidden), lambda i: (i // 2, i % 2, 0, 0, 0)),
+            pl.BlockSpec((1, 2, 2, 64, width), lambda i: (i // 2, i % 2, 0, 0, 0)),
             pl.BlockSpec((2, 48, half), lambda i: (0, 0, 0)),
             pl.BlockSpec((ITEM_ROWS, width), lambda i: (0, 0)),
             pl.BlockSpec((2, 8, part), lambda i: (0, 0, 0)),
@@ -847,11 +847,11 @@
             pl.BlockSpec((rows // steps, width), lambda i: (i, 0)),
             pl.BlockSpec((rows // steps, width), lambda i: (i, 0)),
             pl.BlockSpec((classes, part), lambda i: (0, 0)),
-            pl.BlockSpec((COMPONENTS, 128, part), lambda i: (0, i, 0)),
-            pl.BlockSpec((3, 128, part), lambda i: (0, i, 0)),
-            pl.BlockSpec((32, width), lambda i: (i, 0)),
-            pl.BlockSpec((128, hidden), lambda i: (i, 0)),
-            pl.BlockSpec((128, width), lambda i: (i, 0)),
+            pl.BlockSpec((COMPONENTS, 256, part), lambda i: (0, i, 0)),
+            pl.BlockSpec((3, 256, part), lambda i: (0, i, 0)),
+            pl.BlockSpec((64, width), lambda i: (i, 0)),
+            pl.BlockSpec((256, hidden), lambda i: (i, 0)),
+            pl.BlockSpec((256, width), lambda i: (i, 0)),
         ],
         compiler_params=pltpu.CompilerParams(vmem_limit_bytes=VMEM_BYTES),
     )(

time: 124 us -> 123 us (level)
  Pallas kernels: 123 us -> 121 us
    pallas_call x1, Pallas kernels: 12.4 us -> 10.6 us  [finish(): pl.pallas_call(finish_kernel, grid=(steps,), out_shape=[jax.ShapeDtypeStr...]
where the time goes in v4:
time: 123 us; the launch traced here: 122 us
  Pallas kernels  121 us (98%)
    pallas_call x1, Pallas kernels, on_block(): pl.pallas_call(functools.partial(block_kernel, dims), out_shape=[jax.Shap...  111 us
    pallas_call x1, Pallas kernels, finish(): pl.pallas_call(finish_kernel, grid=(steps,), out_shape=[jax.ShapeDtypeStr...  10.6 us

profile of v4, /device:TPU:0, one launch (start us, length us, event | category | flops | bytes accessed | tf_op | source)
XLA Modules:
  0.0 122.3 jit_solution(828095694220107246)
XLA Ops:
  0.6 110.8 %shard_map.170 = (bf16[4,64,1024]{2,1,0:T(8,128)(2,1)}, bf16[4,64,1024]{2,1,0:T(8,128)(2,1)}, bf16[2,4,2,96,512]{4,3,2,1,0:T(8,128)(2,1)}, bf16[2,4,32,1024]{3,2...) custom-call(bf16[256,1024]{1,0:T(8,128)(2,1)} %refs_0_.1, ...), custom_call_target="tpu_custom_call" | custom-call | flops 10000000000 | bytes 40000000 | tf_op jit(solution)/shard_map/pallas_call | solution.py:885
  111.5 10.6 %shard_map.171 = (bf16[256,1024]{1,0:T(8,128)(2,1)}, bf16[256,1024]{1,0:T(8,128)(2,1)}, f32[1000,256]{1,0:T(8,128)}, f32[6,1024,256]{2,1,0:T(8,128)}, f32[3,1024...) custom-call(s32[3]{0:T(128)} %cls_s.1, ...), custom_call_target="tpu_custom_call" | custom-call | tf_op jit(solution)/shard_map/pallas_call | solution.py:826

commit v5 on v4

--- a/solution.py
+++ b/solution.py
@@ -23,6 +23,7 @@
 GELU_A = math.sqrt(2.0 / math.pi)
 GELU_B = 0.044715
 COPIES = 164
+SENDS = 48
 LOADS = 22
 VMEM_BYTES = 62 * 1024 * 1024
 ITEM_ROWS = 16
@@ -62,10 +63,13 @@
 
     def copy(self, source, target, device, when=None, gets=None):
         k = len(self.made)
+        if k >= SENDS:
+            before, its_when, _ = self.made[k - SENDS]
+            on_some(its_when, before.wait_send)
         one = pltpu.make_async_remote_copy(
             src_ref=source,
             dst_ref=target,
-            send_sem=self.send.at[k],
+            send_sem=self.send.at[k % SENDS],
             recv_sem=self.arrive.at[k],
             device_id=device,
             device_id_type=MESH,
@@ -81,7 +85,8 @@
 
     def finish(self):
         for k, (one, when, _) in enumerate(self.made):
-            on_some(when, one.wait_send)
+            if k >= len(self.made) - SENDS:
+                on_some(when, one.wait_send)
             if k not in self.waited:
                 self.arrived(k)
 
@@ -898,7 +903,7 @@
         in_specs=[anywhere, smem, vmem, vmem] + [anywhere] * 7,
         out_specs=[anywhere] * 9,
         scratch_shapes=[
-            pltpu.SemaphoreType.DMA((COPIES,)),
+            pltpu.SemaphoreType.DMA((SENDS,)),
             pltpu.SemaphoreType.DMA((COPIES,)),
             pltpu.SemaphoreType.DMA((LOADS,)),
             *scratch,

time: 123 us -> 122 us (level)
  no operation moved by 1% of the time
where the time goes in v5:
time: 122 us; the launch traced here: 121 us
  Pallas kernels  120 us (98%)
    pallas_call x1, Pallas kernels, on_block(): pl.pallas_call(functools.partial(block_kernel, dims), out_shape=[jax.Shap...  110 us
    pallas_call x1, Pallas kernels, finish(): pl.pallas_call(finish_kernel, grid=(steps,), out_shape=[jax.ShapeDtypeStr...  10.6 us

profile of v5, /device:TPU:0, one launch (start us, length us, event | category | flops | bytes accessed | tf_op | source)
XLA Modules:
  0.0 121.3 jit_solution(13964971175814488798)
XLA Ops:
  0.6 109.8 %shard_map.170 = (bf16[4,64,1024]{2,1,0:T(8,128)(2,1)}, bf16[4,64,1024]{2,1,0:T(8,128)(2,1)}, bf16[2,4,2,96,512]{4,3,2,1,0:T(8,128)(2,1)}, bf16[2,4,32,1024]{3,2...) custom-call(bf16[256,1024]{1,0:T(8,128)(2,1)} %refs_0_.1, ...), custom_call_target="tpu_custom_call" | custom-call | flops 10000000000 | bytes 40000000 | tf_op jit(solution)/shard_map/pallas_call | solution.py:890
  110.5 10.6 %shard_map.171 = (bf16[256,1024]{1,0:T(8,128)(2,1)}, bf16[256,1024]{1,0:T(8,128)(2,1)}, f32[1000,256]{1,0:T(8,128)}, f32[6,1024,256]{2,1,0:T(8,128)}, f32[3,1024...) custom-call(s32[3]{0:T(128)} %cls_s.1, ...), custom_call_target="tpu_custom_call" | custom-call | tf_op jit(solution)/shard_map/pallas_call | solution.py:831
